TPU v7x, 256 devices: a whole 4x4x8 slice. The times are simulated.
256 devices in a mesh: ctx: 16 (over y_lo, z), chan: 16 (over x, y_hi, core).
Axes of the slice: x: 4, y: 4 (y_hi: 2, y_lo: 2; y = y_hi * 2 + y_lo), z: 8, core: 2. Of those that a mesh axis runs over, the one named last changes fastest.
Arguments:
- query_rows: bfloat16 [4096, 4096], P('ctx', 'chan'), may hold values from -6 to 6
- key_rows: bfloat16 [4096, 4096], P('ctx', 'chan'), may hold values from -6 to 6
- value_rows: bfloat16 [4096, 4096], P('ctx', 'chan'), may hold values from -6 to 6
- residues: float32 [16, 4096], P(None, 'chan'), may hold values from -4 to 4
- decays: float32 [16, 4096], P(None, 'chan'), may hold values from 0.5 to 117
- skip_gain: float32 [4096], P('chan'), may hold values from -4 to 4
- out_weight: bfloat16 [4096, 8192], P('chan'), may hold values from -0.125 to 0.125
- cotangent: bfloat16 [4096, 8192], P('ctx', 'chan'), may hold values from -6 to 6
Outputs:
- layer_out: bfloat16 [4096, 8192], P('ctx', 'chan')
- query_grad: bfloat16 [4096, 4096], P('ctx', 'chan')
- key_grad: bfloat16 [4096, 4096], P('ctx', 'chan')
- value_grad: bfloat16 [4096, 4096], P('ctx', 'chan')
- residue_grad: float32 [16, 4096], P(None, 'chan')
- skip_grad: float32 [4096], P('chan')
- weight_grad: float32 [4096, 8192], P('chan', 'ctx')
All inputs are finite; a program needn't handle non-finite values.
Results may differ from a plain program's by a relative error of at most 0.024.
Values may be sent and summed in bfloat16 or wider, within the bound.
No kernel may reach another device: no remote copies, remote signals or barrier semaphores. Data moves between devices by JAX's collectives and lax.ppermute only.
A program may use at most 128 MiB of HBM per device.

v0:
```python
import functools

import jax
import jax.numpy as jnp
from jax import lax
from jax.experimental import pallas as pl
from jax.experimental.pallas import tpu as pltpu
from jax.sharding import PartitionSpec as P

F32 = jnp.float32
BF16 = jnp.bfloat16
LANES = 128
SUB = 16
HALF = 8
CHIP_MASKS = tuple(range(0, 16, 2))


def traded(value, axis, mask):
    pairs = [(source, source ^ mask) for source in range(lax.axis_size(axis))]
    return lax.ppermute(value, axis, pairs)


def strided(ref, offset, half):
    return ref[pl.ds(offset + half * HALF * SUB, HALF, stride=SUB), :]


def forward_local(key_ref, value_ref, rate_ref, weight_ref, skip_ref, state_ref, mixed_ref, product, carried, scaled):
    product[...] = key_ref[...].astype(F32) * value_ref[...].astype(F32)
    rates = rate_ref[...]
    weights = weight_ref[...]
    pole = jnp.exp(-rates)
    leap = jnp.exp(-float(SUB) * rates)
    state = jnp.zeros_like(rates)
    for block in range(SUB):
        carried[pl.ds(block * SUB, SUB), :] = state
        inner = jnp.broadcast_to(product[pl.ds(block * SUB, 1), :], rates.shape)
        for step in range(1, SUB):
            inner = pole * inner + product[pl.ds(block * SUB + step, 1), :]
        state = leap * state + inner
    state_ref[...] = state
    taps = []
    power = weights
    for step in range(SUB):
        taps.append(jnp.sum(power, axis=0, keepdims=True))
        power = power * pole
        scaled[pl.ds(step * SUB, SUB), :] = power
    taps[0] = taps[0] + skip_ref[...]
    for half in range(2):
        held = [strided(carried, mode, half) for mode in range(SUB)]
        signal = [strided(product, step, half) for step in range(SUB)]
        for step in range(SUB):
            total = taps[0] * signal[step]
            for lag in range(1, step + 1):
                total = total + taps[lag] * signal[step - lag]
            for mode in range(SUB):
                total = total + scaled[pl.ds(step * SUB + mode, 1), :] * held[mode]
            mixed_ref[pl.ds(step + half * HALF * SUB, HALF, stride=SUB), :] = total


def block_decay(rates, mode, half, backward):
    place = lax.broadcasted_iota(jnp.int32, (HALF, LANES), 0).astype(F32) + float(half * HALF)
    distance = float(SUB - 1) - place if backward else place
    return jnp.exp(-float(SUB) * distance * rates[mode : mode + 1, :])


def falling(rates, distance):
    reach = jnp.maximum(distance, 0).astype(F32)
    present = jnp.where(distance >= 0, 1.0, 0.0).astype(F32)
    return jnp.exp(-reach * rates) * present


def near_sums(backward, tokens, position_ref, rate_ref, value_refs, inside_ref, whole_ref):
    values = [ref[...] for ref in value_refs]
    rates = rate_ref[...]
    modes = rates.shape[0]
    low = position_ref[1] & 3
    inside = jnp.zeros_like(rates)
    whole = jnp.zeros_like(rates)
    for mask in range(4):
        spot = low ^ mask
        state = values[mask][:modes]
        gap = spot - low - 1 if backward else low - 1 - spot
        far = spot if backward else 3 - spot
        inside = inside + falling(rates, tokens * gap) * state
        whole = whole + falling(rates, tokens * far) * state
    inside_ref[...] = inside
    whole_ref[pl.ds(0, modes), :] = whole
    if values[0].shape[0] > modes:
        sums = [value[modes:] for value in values]
        whole_ref[pl.ds(modes, sums[0].shape[0]), :] = (sums[0] + sums[1]) + (sums[2] + sums[3])


def forward_near(tokens, position_ref, rate_ref, *rest):
    own_ref, arrived_ref, inside_ref, whole_ref, pair_ref = rest[4:]
    near_sums(False, tokens, position_ref, rate_ref, rest[:4], inside_ref, whole_ref)
    pair_ref[0] = own_ref[...]
    pair_ref[1] = arrived_ref[...]


def open_far(first_ref, third_ref, even_ref, odd_ref):
    even_ref[...] = first_ref[0]
    odd_ref[...] = third_ref[1]


def stack_blocks(refs, out_ref):
    pair, first, third, even, odd = refs
    for index, block in enumerate((pair.at[0], pair.at[1], first.at[0], first.at[1])):
        out_ref[index] = block[...]
    for index, block in enumerate((even, odd, third.at[0], third.at[1])):
        out_ref[4 + index] = block[...]


def joined(backward, tokens, position_ref, rates, inside, across):
    low = position_ref[1] & 3
    high = lax.shift_right_logical(position_ref[1], 2)
    total = jnp.zeros_like(rates)
    for mask in range(1, 4):
        spot = high ^ mask
        gap = spot - high - 1 if backward else high - 1 - spot
        total = total + falling(rates, 4 * tokens * gap) * across[mask - 1]
    span = 3 - low if backward else low
    return inside + falling(rates, tokens * span) * total


def forward_mix(position_ref, local_ref, query_ref, rate_ref, weight_ref, inside_ref, first_ref, second_ref, third_ref, mixed_ref, gated_ref, turned_ref, entering_ref, scaled, narrow):
    tokens = local_ref.shape[0]
    for tile in range(2):
        lanes = pl.ds(tile * LANES, LANES)
        narrow[...] = local_ref[:, lanes]
        rates = rate_ref[:, lanes]
        weights = weight_ref[:, lanes]
        across = [ref[:, lanes] for ref in (first_ref, second_ref, third_ref)]
        entering = joined(False, tokens, position_ref, rates, inside_ref[:, lanes], across)
        entering_ref[:, lanes] = entering
        pole = jnp.exp(-rates)
        power = weights
        for step in range(SUB):
            power = power * pole
            scaled[pl.ds(step * SUB, SUB), :] = power
        for half in range(2):
            held = [
                block_decay(rates, mode, half, False) * entering[mode : mode + 1, :]
                for mode in range(SUB)
            ]
            for step in range(SUB):
                rows = pl.ds(step + half * HALF * SUB, HALF, stride=SUB)
                total = narrow[rows, :]
                for mode in range(SUB):
                    total = total + scaled[pl.ds(step * SUB + mode, 1), :] * held[mode]
                narrow[rows, :] = total
        mixed_ref[:, lanes] = narrow[...]
    gated = query_ref[...].astype(F32) * mixed_ref[...]
    gated_ref[...] = gated.astype(BF16)
    turned_ref[...] = gated.T.astype(BF16)


def stack_arrived(*refs):
    stack_blocks(refs[:5], refs[5])


def weight_part(position_ref, turned_ref, own_ref, other_ref, out_ref, token_ref):
    place = position_ref[0]
    block = own_ref.shape[2]
    for ref, flip in ((own_ref, 0), (other_ref, 1)):
        for index, mask in enumerate(CHIP_MASKS):
            first = pl.multiple_of((place ^ (mask | flip)) * block, block)
            out_ref[:, pl.ds(first, block)] = jnp.dot(
                turned_ref[...], ref[index], preferred_element_type=F32
            ).astype(BF16)
    token_ref[...] = jnp.zeros(token_ref.shape, F32)


def project_rows(position_ref, query_ref, mixed_ref, gated_ref, out_weight_ref, own_ref, other_ref, query_grad_ref, drive_ref, sent_ref, mine_ref):
    place = position_ref[0]
    block = own_ref.shape[2]
    total = jnp.zeros(query_ref.shape, F32)
    for ref, flip, part_ref in ((other_ref, 1, sent_ref), (own_ref, 0, mine_ref)):
        for index, mask in enumerate(CHIP_MASKS):
            first = pl.multiple_of((place ^ (mask | flip)) * block, block)
            columns = out_weight_ref[:, pl.ds(first, block)]
            total = total + lax.dot_general(
                ref[index], columns, (((1,), (1,)), ((), ())), preferred_element_type=F32
            )
            part_ref[index] = jnp.dot(
                gated_ref[...], columns, preferred_element_type=F32
            ).astype(BF16)
    query_grad_ref[...] = (total * mixed_ref[...]).astype(BF16)
    drive_ref[...] = total * query_ref[...].astype(F32)


def backward_local(drive_ref, key_ref, value_ref, rate_ref, weight_ref, gain_ref, skip_ref, entering_ref, local_ref, sums_ref, product, carried):
    product[...] = key_ref[...].astype(F32) * value_ref[...].astype(F32)
    rates = rate_ref[...]
    weights = weight_ref[...]
    pole = jnp.exp(-rates)
    leap = jnp.exp(-float(SUB) * rates)
    state = jnp.zeros_like(rates)
    for block in reversed(range(SUB)):
        carried[pl.ds(block * SUB, SUB), :] = state
        inner = jnp.broadcast_to(drive_ref[pl.ds(block * SUB + SUB - 1, 1), :], rates.shape)
        for step in reversed(range(SUB - 1)):
            inner = pole * inner + drive_ref[pl.ds(block * SUB + step, 1), :]
        state = leap * state + inner
    sums_ref[pl.ds(0, SUB), :] = state
    sums_ref[pl.ds(SUB, SUB), :] = pole * entering_ref[...] * state
    sums_ref[pl.ds(2 * SUB, HALF), :] = jnp.zeros((HALF, LANES), F32)
    for half in range(2):
        drives = [strided(drive_ref, step, half) for step in range(SUB)]
        signal = [strided(product, step, half) for step in range(SUB)]
        totals = [skip_ref[...] * drive for drive in drives]
        direct = drives[0] * signal[0]
        for step in range(1, SUB):
            direct = direct + drives[step] * signal[step]
        sums_ref[pl.ds(2 * SUB, 1), :] += jnp.sum(direct, axis=0, keepdims=True)
        for mode in range(SUB):
            running = strided(carried, mode, half)
            gathered = jnp.zeros_like(running)
            for step in reversed(range(SUB)):
                running = pole[mode : mode + 1, :] * running + drives[step]
                totals[step] = totals[step] + weights[mode : mode + 1, :] * running
                gathered = gathered + signal[step] * running
            sums_ref[pl.ds(SUB + mode, 1), :] += jnp.sum(gathered, axis=0, keepdims=True)
        for step in range(SUB):
            local_ref[pl.ds(step + half * HALF * SUB, HALF, stride=SUB), :] = totals[step]
    sums_ref[pl.ds(SUB, SUB), :] *= gain_ref[...]


def backward_mix(position_ref, local_ref, key_ref, value_ref, rate_ref, weight_ref, inside_ref, whole_ref, first_ref, second_ref, third_ref, key_grad_ref, value_grad_ref, residue_ref, skip_sum_ref, scaled, grads):
    rates = rate_ref[...]
    tokens = local_ref.shape[0]
    across = [ref[pl.ds(0, SUB), :] for ref in (first_ref, second_ref, third_ref)]
    later = joined(True, tokens, position_ref, rates, inside_ref[...], across)
    pole = jnp.exp(-rates)
    power = weight_ref[...]
    for step in reversed(range(SUB)):
        power = power * pole
        scaled[pl.ds(step * SUB, SUB), :] = power
    for half in range(2):
        held = [
            block_decay(rates, mode, half, True) * later[mode : mode + 1, :] for mode in range(SUB)
        ]
        for step in range(SUB):
            total = strided(local_ref, step, half)
            for mode in range(SUB):
                total = total + scaled[pl.ds(step * SUB + mode, 1), :] * held[mode]
            grads[pl.ds(step + half * HALF * SUB, HALF, stride=SUB), :] = total
    product_grad = grads[...]
    key_grad_ref[...] = (product_grad * value_ref[...].astype(F32)).astype(BF16)
    value_grad_ref[...] = (product_grad * key_ref[...].astype(F32)).astype(BF16)
    for first, count, ref in ((SUB, SUB, residue_ref), (2 * SUB, 1, skip_sum_ref)):
        part = pl.ds(first, count)
        ref[...] = (whole_ref[part, :] + first_ref[part, :]) + (
            second_ref[part, :] + third_ref[part, :]
        )


def widened(ref, *place):
    return ref[place].astype(F32) if place else ref[...].astype(F32)


def merge_cores(mine_ref, other_ref, even_ref, odd_ref, rest_ref):
    for index, mask in enumerate(CHIP_MASKS):
        total = (widened(mine_ref, index) + widened(other_ref, index)).astype(BF16)
        if mask == 8:
            even_ref[...] = total
        elif mask == 10:
            odd_ref[...] = total
        else:
            rest_ref[index if mask < 8 else index - 2] = total


def merge_far(rest_ref, even_ref, odd_ref, first_ref, third_ref):
    first_ref[0] = rest_ref[2]
    first_ref[1] = (widened(rest_ref, 3) + widened(odd_ref)).astype(BF16)
    third_ref[0] = (widened(rest_ref, 4) + widened(even_ref)).astype(BF16)
    third_ref[1] = rest_ref[5]


def backward_near(tokens, position_ref, rate_ref, *rest):
    near_sums(True, tokens, position_ref, rate_ref, rest[:4], rest[4], rest[5])


def merge_near(rest_ref, first_ref, third_ref, kept_ref, sent_ref):
    for index, ref in enumerate((kept_ref, sent_ref)):
        total = widened(rest_ref, index) + widened(first_ref, index) + widened(third_ref, index)
        ref[...] = total.astype(ref.dtype)


def merge_last(kept_ref, arrived_ref, out_ref):
    out_ref[...] = (kept_ref[...] + widened(arrived_ref)).astype(BF16)


VMEM = pl.BlockSpec(memory_space=pltpu.VMEM)
SMEM = pl.BlockSpec(memory_space=pltpu.SMEM)
ANY = pl.BlockSpec(memory_space=pl.ANY)


def tile_of(rows):
    return pl.BlockSpec((rows, LANES), lambda tile: (0, tile))


def shape_of(rows, columns, kind=F32):
    return jax.ShapeDtypeStruct((rows, columns), kind)


def ordered_call(body, ordered, in_specs, *operands, **options):
    count = len(ordered)

    def skipping(*refs):
        body(*refs[count:])

    return pl.pallas_call(skipping, in_specs=[ANY] * count + in_specs, **options)(
        *ordered, *operands
    )


def granted(mebibytes):
    return pltpu.CompilerParams(vmem_limit_bytes=mebibytes * 1024 * 1024)


def kind_of(*shape, dtype=BF16):
    return jax.ShapeDtypeStruct(shape, dtype)


def local_call(body, out_shape, *operands, ordered=(), scalars=0, scratch=(), limit=11):
    plain = body.func if isinstance(body, functools.partial) else body
    return ordered_call(
        body,
        ordered,
        [SMEM] * scalars
        + [VMEM] * (len(operands) - scalars),
        *operands,
        out_specs=[VMEM] * len(out_shape),
        out_shape=out_shape,
        scratch_shapes=scratch,
        compiler_params=granted(limit),
        name=plain.__name__,
    )


def on_device(query_rows, key_rows, value_rows, residues, decays, skip_gain, out_weight, cotangent):
    tokens, width = query_rows.shape
    modes = residues.shape[0]
    ctx_count = lax.axis_size("ctx")
    chan_count = lax.axis_size("chan")
    positions = jnp.stack([lax.axis_index("chan"), lax.axis_index("ctx")]).astype(jnp.int32)
    rates = decays / (tokens * ctx_count)
    gains = jnp.sqrt(-jnp.expm1(-2.0 * rates) / modes)
    weights = residues * gains
    skip_row = skip_gain.reshape(1, width)
    tiles = width // LANES
    rows = tile_of(tokens)
    few = tile_of(modes)
    one = tile_of(1)
    tall = 2 * modes + HALF
    sums = tile_of(tall)
    block_scratch = pltpu.VMEM((tokens, LANES), F32)
    columns = cotangent.shape[1]
    block = kind_of(tokens, columns)
    pair_block = kind_of(2, tokens, columns)
    eight = kind_of(8, tokens, columns)
    square = shape_of(tokens, width)
    state_shape = shape_of(modes, width)
    tall_shape = shape_of(tall, width)

    arrived = traded(cotangent, "chan", 2)
    state, local = pl.pallas_call(
        forward_local,
        grid=(tiles,),
        in_specs=[rows, rows, few, few, one],
        out_specs=[few, rows],
        out_shape=[state_shape, square],
        scratch_shapes=[block_scratch] * 3,
        name="forward_local",
    )(key_rows, value_rows, rates, weights, skip_row)
    near = [state] + [traded(state, "ctx", mask) for mask in (1, 2, 3)]
    inside, whole, pair = local_call(
        functools.partial(forward_near, tokens),
        [state_shape, state_shape, pair_block],
        positions,
        rates,
        *near,
        cotangent,
        arrived,
        scalars=1,
    )

    first, third = traded(pair, "chan", 4), traded(pair, "chan", 12)
    across = [traded(whole, "ctx", 4 * mask) for mask in (1, 2, 3)]
    far = local_call(open_far, [block, block], first, third, ordered=across)
    mixed, gated, gated_turned, entering = local_call(
        forward_mix,
        [square, kind_of(tokens, width), kind_of(width, tokens), state_shape],
        positions,
        local,
        query_rows,
        rates,
        weights,
        inside,
        *across,
        ordered=far[:1],
        scalars=1,
        scratch=[block_scratch] * 2,
    )

    even, odd = traded(far[0], "chan", 12), traded(far[1], "chan", 4)
    own = local_call(stack_arrived, [eight], pair, first, third, even, odd)[0]

    sibling = traded(own, "chan", 1)
    weight_share, token = local_call(
        weight_part,
        [kind_of(width, chan_count * columns), shape_of(HALF, LANES)],
        positions,
        gated_turned,
        own,
        sibling,
        scalars=1,
    )
    weight_grad = lax.psum_scatter(weight_share, "ctx", scatter_dimension=1, tiled=True)
    query_grad, drive, other, mine = local_call(
        project_rows,
        [kind_of(tokens, width), square, eight, eight],
        positions,
        query_rows,
        mixed,
        gated,
        out_weight,
        own,
        sibling,
        ordered=[token],
        scalars=1,
        limit=14,
    )
    back_local, back_state = pl.pallas_call(
        backward_local,
        grid=(tiles,),
        in_specs=[rows, rows, rows, few, few, few, one, few],
        out_specs=[rows, sums],
        out_shape=[square, tall_shape],
        scratch_shapes=[block_scratch] * 2,
        name="backward_local",
    )(drive, key_rows, value_rows, rates, weights, gains, skip_row, entering)
    even, odd, rest = local_call(
        merge_cores,
        [block, block, kind_of(6, tokens, columns)],
        mine,
        traded(other, "chan", 1),
        ordered=[back_state],
    )

    near = [back_state] + [traded(back_state, "ctx", mask) for mask in (1, 2, 3)]
    inside, whole = local_call(
        functools.partial(backward_near, tokens),
        [state_shape, tall_shape],
        positions,
        rates,
        *near,
        scalars=1,
    )
    first, third = local_call(
        merge_far,
        [pair_block, pair_block],
        rest,
        traded(even, "chan", 4),
        traded(odd, "chan", 12),
        ordered=[whole],
    )

    across = [traded(whole, "ctx", 4 * mask) for mask in (1, 2, 3)]
    kept, sent = local_call(
        merge_near,
        [shape_of(tokens, columns), block],
        rest,
        traded(first, "chan", 4),
        traded(third, "chan", 12),
        ordered=across,
    )

    layer_out = local_call(
        merge_last, [kind_of(tokens, columns)], kept, traded(sent, "chan", 2)
    )[0]
    key_grad, value_grad, residue_grad, skip_sum = pl.pallas_call(
        backward_mix,
        grid=(tiles,),
        in_specs=[SMEM, rows, rows, rows, few, few, few] + [sums] * 4,
        out_specs=[rows, rows, few, one],
        out_shape=[
            kind_of(tokens, width),
            kind_of(tokens, width),
            state_shape,
            shape_of(1, width),
        ],
        scratch_shapes=[block_scratch] * 2,
        name="backward_mix",
    )(positions, back_local, key_rows, value_rows, rates, weights, inside, whole, *across)
    return (
        layer_out,
        query_grad,
        key_grad,
        value_grad,
        residue_grad,
        skip_sum.reshape(width),
        weight_grad.astype(F32),
    )


def solution(mesh):
    placed = (
        P("ctx", "chan"),
        P("ctx", "chan"),
        P("ctx", "chan"),
        P(None, "chan"),
        P(None, "chan"),
        P("chan"),
        P("chan", None),
        P("ctx", "chan"),
    )
    return jax.shard_map(
        on_device,
        mesh=mesh,
        in_specs=placed,
        out_specs=(
            P("ctx", "chan"),
            P("ctx", "chan"),
            P("ctx", "chan"),
            P("ctx", "chan"),
            P(None, "chan"),
            P("chan"),
            P("chan", "ctx"),
        ),
        check_vma=False,
    )
```

profile of v0, /device:TPU:14, one launch (start us, length us, event | category | flops | bytes accessed | tf_op | source)
XLA Modules:
  0.0 144.3 jit_solution(2898314450557201131)
XLA Ops:
  7.2 2.4 %collective-permute-start.3 = (bf16[256,512]{1,0:T(8,128)(2,1)}, bf16[256,512]{1,0:T(8,128)(2,1)S(1)}, u32[]{:S(2)}, u32[]{:S(2)}) collective-permute-start(bf16[256,512]{1,0:T(8,128)(2,1)} %refs_6_.1), channel_id=1, source_target_pairs={{0,2},{1,3},{2,0},{3,1},{4,6},{5,7},{6,4},{7,5},{8,10},{9,11},{10,... | collective-permute-start | bytes 786440 | tf_op jit(solution)/shard_map/ppermute | solution.py:20
  11.0 2.5 %forward_local.1 = (f32[16,256]{1,0:T(8,128)}, f32[256,256]{1,0:T(8,128)}) custom-call(bf16[256,256]{1,0:T(8,128)(2,1)} %key_ref.5, bf16[256,256]{1,0:T(8,128)(2,1)} %value_ref.5, f32[16,256]{1,0:T(8,128)} %get-tuple-element.73.rate_ref.refs_1_.refs_4_, f32[16,256]{1,0:T(8,128)} %get-tuple-element.72.weight_ref.refs_5_, f32[1,256]{1,0:T(1,128)} %bitcast.4), custom_call_target="tpu_custom_call" | custom-call | tf_op jit(solution)/shard_map/forward_local/pallas_call | solution.py:367
  13.5 4.6 %collective-permute-start.2 = (f32[16,256]{1,0:T(8,128)}, f32[16,256]{1,0:T(8,128)S(1)}, u32[]{:S(2)}, u32[]{:S(2)}) collective-permute-start(f32[16,256]{1,0:T(8,128)} %get-tuple-element.39.refs_2_), channel_id=1, source_target_pairs={{0,48},{16,32},{32,16},{48,0},{64,112},{80,96},{96,80},{112,64},{1... | collective-permute-start | bytes 49160 | tf_op jit(solution)/shard_map/ppermute | solution.py:20
  20.1 2.9 %collective-permute-done.1.refs_4_ = f32[16,256]{1,0:T(8,128)S(1)} collective-permute-done((f32[16,256]{1,0:T(8,128)}, f32[16,256]{1,0:T(8,128)S(1)}, u32[]{:S(2)}, u32[]{:S(2)}) %collective-permute-start.1) | collective-permute-done | bytes 16416 | tf_op jit(solution)/shard_map/ppermute | solution.py:20
  27.4 5.3 %collective-permute-start.6 = (f32[16,256]{1,0:T(8,128)S(1)}, f32[16,256]{1,0:T(8,128)S(1)}, u32[]{:S(2)}, u32[]{:S(2)}) collective-permute-start(f32[16,256]{1,0:T(8,128)S(1)} %get-tuple-element.40), channel_id=1, source_target_pairs={{0,192},{16,208},{32,224},{48,240},{64,128},{80,144},{96,160},{112... | collective-permute-start | bytes 49160 | tf_op jit(solution)/shard_map/ppermute | solution.py:20
  36.4 4.6 %collective-permute-done.4.refs_0_.refs_7_ = f32[16,256]{1,0:T(8,128)S(1)} collective-permute-done((f32[16,256]{1,0:T(8,128)S(1)}, f32[16,256]{1,0:T(8,128)S(1)}, u32[]{:S(2)}, u32[]{:S(2)}) %collective-permute-start.4) | collective-permute-done | bytes 16416 | tf_op jit(solution)/shard_map/ppermute | solution.py:20
  42.3 2.8 %collective-permute-start.9 = (bf16[256,512]{1,0:T(8,128)(2,1)S(1)}, bf16[256,512]{1,0:T(8,128)(2,1)S(1)}, u32[]{:S(2)}, u32[]{:S(2)}) collective-permute-start(bf16[256,512]{1,0:T(8,128)(2,1)S(1)} %get-tuple-element.42.refs_0_), channel_id=1, source_target_pairs={{0,12},{1,13},{2,14},{3,15},{4,8},{5,9},{6,10},{7,11},{8,4},{9,5},... | collective-permute-start | bytes 786440 | tf_op jit(solution)/shard_map/ppermute | solution.py:20
  45.1 2.4 %collective-permute-done.10.refs_4_ = bf16[256,512]{1,0:T(8,128)(2,1)S(1)} collective-permute-done((bf16[256,512]{1,0:T(8,128)(2,1)S(1)}, bf16[256,512]{1,0:T(8,128)(2,1)S(1)}, u32[]{:S(2)}, u32[]{:S(2)}) %collective-permute-start.10) | collective-permute-done | bytes 262176 | tf_op jit(solution)/shard_map/ppermute | solution.py:20
  47.5 2.4 %collective-permute-done.9.refs_3_ = bf16[256,512]{1,0:T(8,128)(2,1)S(1)} collective-permute-done((bf16[256,512]{1,0:T(8,128)(2,1)S(1)}, bf16[256,512]{1,0:T(8,128)(2,1)S(1)}, u32[]{:S(2)}, u32[]{:S(2)}) %collective-permute-start.9) | collective-permute-done | bytes 262176 | tf_op jit(solution)/shard_map/ppermute | solution.py:20
  52.1 2.2 %collective-permute-done.11.refs_3_.refs_7_ = bf16[8,256,512]{2,1,0:T(8,128)(2,1)S(1)} collective-permute-done((bf16[8,256,512]{2,1,0:T(8,128)(2,1)S(1)}, bf16[8,256,512]{2,1,0:T(8,128)(2,1)S(1)}, u32[]{:S(2)}, u32[]{:S(2)}) %collective-permute-start.11) | collective-permute-done | bytes 2097184 | tf_op jit(solution)/shard_map/ppermute | solution.py:20
  56.2 2.0 %copy-done.3 = bf16[256,8192]{1,0:T(8,128)(2,1)} copy-done((bf16[256,8192]{1,0:T(8,128)(2,1)}, bf16[256,8192]{1,0:T(8,128)(2,1)S(1)}, u32[]{:S(2)}) %copy-start.3) | copy-done | bytes 4194328
  59.8 2.2 %copy-done.2 = bf16[256,8192]{1,0:T(8,128)(2,1)S(1)} copy-done((bf16[256,8192]{1,0:T(8,128)(2,1)S(1)}, bf16[256,8192]{1,0:T(8,128)(2,1)}, u32[]{:S(2)}) %copy-start.2) | copy-done | bytes 4194328
  61.9 4.1 %project_rows.1 = (bf16[256,256]{1,0:T(8,128)(2,1)}, f32[256,256]{1,0:T(8,128)S(1)}, bf16[8,256,512]{2,1,0:T(8,128)(2,1)}, bf16[8,256,512]{2,1,0:T(8,128)(2,1)S(1)}) custom-call(f32[8,128]{1,0:T(8,128)S(1)} %get-tuple-element.47.refs_0_, s32[2]{0:T(128)S(1)} %pad_add_fusion.refs_0_.refs_1_.position_ref, bf16[256,256]{1,0:T(8,128)(2,1)S(1)} %copy-done.9, ...), custom_call_target="tpu_custom_call" | custom-call | tf_op jit(solution)/shard_map/project_rows/pallas_call | solution.py:312
  68.2 3.1 %backward_local.1 = (f32[256,256]{1,0:T(8,128)}, f32[40,256]{1,0:T(8,128)}) custom-call(f32[256,256]{1,0:T(8,128)} %copy-done.13, bf16[256,256]{1,0:T(8,128)(2,1)} %key_ref.5, bf16[256,256]{1,0:T(8,128)(2,1)} %value_ref.5, f32[16,256]{1,0:T(8,128)} %get-tuple-element.73.rate_ref.refs_1_.refs_4_, f32[16,256]{1,0:T(8,128)} %get-tuple-element.72.weight_ref.refs_5_, ...), custom_call_target="tpu_custom_call" | custom-call | tf_op jit(solution)/shard_map/backward_local/pallas_call | solution.py:434
  75.4 2.8 %collective-permute-start.20 = (bf16[256,512]{1,0:T(8,128)(2,1)S(1)}, bf16[256,512]{1,0:T(8,128)(2,1)S(1)}, u32[]{:S(2)}, u32[]{:S(2)}) collective-permute-start(bf16[256,512]{1,0:T(8,128)(2,1)S(1)} %get-tuple-element.58), channel_id=1, source_target_pairs={{0,12},{1,13},{2,14},{3,15},{4,8},{5,9},{6,10},{7,11},{8,4},{9,5},... | collective-permute-start | bytes 786440 | tf_op jit(solution)/shard_map/ppermute | solution.py:20
  82.7 2.5 %collective-permute-done.14.refs_5_ = f32[40,256]{1,0:T(8,128)S(1)} collective-permute-done((f32[40,256]{1,0:T(8,128)S(1)}, f32[40,256]{1,0:T(8,128)S(1)}, u32[]{:S(2)}, u32[]{:S(2)}) %collective-permute-start.14) | collective-permute-done | bytes 40992 | tf_op jit(solution)/shard_map/ppermute | solution.py:20
  85.2 2.4 %collective-permute-done.13.refs_4_ = f32[40,256]{1,0:T(8,128)S(1)} collective-permute-done((f32[40,256]{1,0:T(8,128)S(1)}, f32[40,256]{1,0:T(8,128)S(1)}, u32[]{:S(2)}, u32[]{:S(2)}) %collective-permute-start.13) | collective-permute-done | bytes 40992 | tf_op jit(solution)/shard_map/ppermute | solution.py:20
  90.9 2.0 %collective-permute-start.17 = (f32[40,256]{1,0:T(8,128)S(1)}, f32[40,256]{1,0:T(8,128)S(1)}, u32[]{:S(2)}, u32[]{:S(2)}) collective-permute-start(f32[40,256]{1,0:T(8,128)S(1)} %get-tuple-element.53.refs_0_.whole_ref), channel_id=1, source_target_pairs={{0,192},{16,208},{32,224},{48,240},{64,128},{80,144},{96,160},{112... | collective-permute-start | bytes 122888 | tf_op jit(solution)/shard_map/ppermute | solution.py:20
  93.7 4.6 %collective-permute-start.15 = (f32[40,256]{1,0:T(8,128)S(1)}, f32[40,256]{1,0:T(8,128)S(1)}, u32[]{:S(2)}, u32[]{:S(2)}) collective-permute-start(f32[40,256]{1,0:T(8,128)S(1)} %get-tuple-element.53.refs_0_.whole_ref), channel_id=1, source_target_pairs={{0,64},{16,80},{32,96},{48,112},{64,0},{80,16},{96,32},{112,48},{1... | collective-permute-start | bytes 122888 | tf_op jit(solution)/shard_map/ppermute | solution.py:20
  98.3 2.4 %collective-permute-done.17.refs_2_.third_ref = f32[40,256]{1,0:T(8,128)S(1)} collective-permute-done((f32[40,256]{1,0:T(8,128)S(1)}, f32[40,256]{1,0:T(8,128)S(1)}, u32[]{:S(2)}, u32[]{:S(2)}) %collective-permute-start.17) | collective-permute-done | bytes 40992 | tf_op jit(solution)/shard_map/ppermute | solution.py:20
  100.7 2.1 %collective-permute-done.15.refs_0_.first_ref = f32[40,256]{1,0:T(8,128)S(1)} collective-permute-done((f32[40,256]{1,0:T(8,128)S(1)}, f32[40,256]{1,0:T(8,128)S(1)}, u32[]{:S(2)}, u32[]{:S(2)}) %collective-permute-start.15) | collective-permute-done | bytes 40992 | tf_op jit(solution)/shard_map/ppermute | solution.py:20
  105.3 2.2 %backward_mix.1 = (bf16[256,256]{1,0:T(8,128)(2,1)}, bf16[256,256]{1,0:T(8,128)(2,1)}, f32[16,256]{1,0:T(8,128)}, f32[1,256]{1,0:T(1,128)}) custom-call(s32[2]{0:T(128)} %copy-done.19, f32[256,256]{1,0:T(8,128)} %get-tuple-element.64.local_ref, bf16[256,256]{1,0:T(8,128)(2,1)} %key_ref.5, bf16[256,256]{1,0:T(8,128)(2,1)} %value_ref.5, ...), custom_call_target="tpu_custom_call" | custom-call | tf_op jit(solution)/shard_map/backward_mix/pallas_call | solution.py:482
  107.5 16.7 %collective-permute-done.23.refs_1_ = bf16[256,512]{1,0:T(8,128)(2,1)S(1)} collective-permute-done((bf16[256,512]{1,0:T(8,128)(2,1)S(1)}, bf16[256,512]{1,0:T(8,128)(2,1)S(1)}, u32[]{:S(2)}, u32[]{:S(2)}) %collective-permute-start.23) | collective-permute-done | bytes 262176 | tf_op jit(solution)/shard_map/ppermute | solution.py:20
  125.0 10.7 %reduce-scatter.2.cloned.1.call-done = bf16[256,512]{1,0:T(8,128)(2,1)} async-done(((bf16[256,8192]{1,0:T(8,128)(2,1)}), bf16[256,512]{1,0:T(8,128)(2,1)}) %reduce-scatter.2.cloned.1.call-update) | async-done | bytes 262160 | tf_op jit(solution)/shard_map/reduce_scatter | solution.py:419
  (90 shorter events, 38.2 us)
Async XLA Ops:
  7.2 128.5 %reduce-scatter.2.cloned.1.call-start = ((), (), s32[]{:S(2)}) async-start(), calls=%async_computation.1 | async-start | bytes 4456448 | tf_op jit(solution)/shard_map/reduce_scatter | solution.py:419
  7.2 15.7 %collective-permute-start.3 = (bf16[256,512]{1,0:T(8,128)(2,1)}, bf16[256,512]{1,0:T(8,128)(2,1)S(1)}, u32[]{:S(2)}, u32[]{:S(2)}) collective-permute-start(bf16[256,512]{1,0:T(8,128)(2,1)} %refs_6_.1), channel_id=1, source_target_pairs={{0,2},{1,3},{2,0},{3,1},{4,6},{5,7},{6,4},{7,5},{8,10},{9,11},{10,... | collective-permute-start | bytes 786440 | tf_op jit(solution)/shard_map/ppermute | solution.py:20
  13.5 6.6 %collective-permute-start.2 = (f32[16,256]{1,0:T(8,128)}, f32[16,256]{1,0:T(8,128)S(1)}, u32[]{:S(2)}, u32[]{:S(2)}) collective-permute-start(f32[16,256]{1,0:T(8,128)} %get-tuple-element.39.refs_2_), channel_id=1, source_target_pairs={{0,48},{16,32},{32,16},{48,0},{64,112},{80,96},{96,80},{112,64},{1... | collective-permute-start | bytes 49160 | tf_op jit(solution)/shard_map/ppermute | solution.py:20
  18.1 4.8 %collective-permute-start.1 = (f32[16,256]{1,0:T(8,128)}, f32[16,256]{1,0:T(8,128)S(1)}, u32[]{:S(2)}, u32[]{:S(2)}) collective-permute-start(f32[16,256]{1,0:T(8,128)} %get-tuple-element.39.refs_2_), channel_id=1, source_target_pairs={{0,32},{16,48},{32,0},{48,16},{64,96},{80,112},{96,64},{112,80},{1... | collective-permute-start | bytes 49160 | tf_op jit(solution)/shard_map/ppermute | solution.py:20
  18.1 4.8 %collective-permute-start = (f32[16,256]{1,0:T(8,128)}, f32[16,256]{1,0:T(8,128)S(1)}, u32[]{:S(2)}, u32[]{:S(2)}) collective-permute-start(f32[16,256]{1,0:T(8,128)} %get-tuple-element.39.refs_2_), channel_id=1, source_target_pairs={{0,16},{16,0},{32,48},{48,32},{64,80},{80,64},{96,112},{112,96},{1... | collective-permute-start | bytes 49160 | tf_op jit(solution)/shard_map/ppermute | solution.py:20
  25.9 15.1 %collective-permute-start.8 = (bf16[2,256,512]{2,1,0:T(8,128)(2,1)S(1)}, bf16[2,256,512]{2,1,0:T(8,128)(2,1)S(1)}, u32[]{:S(2)}, u32[]{:S(2)}) collective-permute-start(bf16[2,256,512]{2,1,0:T(8,128)(2,1)S(1)} %get-tuple-element.41.refs_0_), channel_id=1, source_target_pairs={{0,12},{1,13},{2,14},{3,15},{4,8},{5,9},{6,10},{7,11},{8,4},{9,5},... | collective-permute-start | bytes 1572872 | tf_op jit(solution)/shard_map/ppermute | solution.py:20
  26.5 14.5 %collective-permute-start.7 = (bf16[2,256,512]{2,1,0:T(8,128)(2,1)S(1)}, bf16[2,256,512]{2,1,0:T(8,128)(2,1)S(1)}, u32[]{:S(2)}, u32[]{:S(2)}) collective-permute-start(bf16[2,256,512]{2,1,0:T(8,128)(2,1)S(1)} %get-tuple-element.41.refs_0_), channel_id=1, source_target_pairs={{0,4},{1,5},{2,6},{3,7},{4,0},{5,1},{6,2},{7,3},{8,12},{9,13},{10,... | collective-permute-start | bytes 1572872 | tf_op jit(solution)/shard_map/ppermute | solution.py:20
  27.4 8.7 %collective-permute-start.6 = (f32[16,256]{1,0:T(8,128)S(1)}, f32[16,256]{1,0:T(8,128)S(1)}, u32[]{:S(2)}, u32[]{:S(2)}) collective-permute-start(f32[16,256]{1,0:T(8,128)S(1)} %get-tuple-element.40), channel_id=1, source_target_pairs={{0,192},{16,208},{32,224},{48,240},{64,128},{80,144},{96,160},{112... | collective-permute-start | bytes 49160 | tf_op jit(solution)/shard_map/ppermute | solution.py:20
  33.3 7.6 %collective-permute-start.4 = (f32[16,256]{1,0:T(8,128)S(1)}, f32[16,256]{1,0:T(8,128)S(1)}, u32[]{:S(2)}, u32[]{:S(2)}) collective-permute-start(f32[16,256]{1,0:T(8,128)S(1)} %get-tuple-element.40), channel_id=1, source_target_pairs={{0,64},{16,80},{32,96},{48,112},{64,0},{80,16},{96,32},{112,48},{1... | collective-permute-start | bytes 49160 | tf_op jit(solution)/shard_map/ppermute | solution.py:20
  41.0 6.5 %collective-permute-start.10 = (bf16[256,512]{1,0:T(8,128)(2,1)S(1)}, bf16[256,512]{1,0:T(8,128)(2,1)S(1)}, u32[]{:S(2)}, u32[]{:S(2)}) collective-permute-start(bf16[256,512]{1,0:T(8,128)(2,1)S(1)} %get-tuple-element.46), channel_id=1, source_target_pairs={{0,4},{1,5},{2,6},{3,7},{4,0},{5,1},{6,2},{7,3},{8,12},{9,13},{10,... | collective-permute-start | bytes 786440 | tf_op jit(solution)/shard_map/ppermute | solution.py:20
  42.3 7.7 %collective-permute-start.9 = (bf16[256,512]{1,0:T(8,128)(2,1)S(1)}, bf16[256,512]{1,0:T(8,128)(2,1)S(1)}, u32[]{:S(2)}, u32[]{:S(2)}) collective-permute-start(bf16[256,512]{1,0:T(8,128)(2,1)S(1)} %get-tuple-element.42.refs_0_), channel_id=1, source_target_pairs={{0,12},{1,13},{2,14},{3,15},{4,8},{5,9},{6,10},{7,11},{8,4},{9,5},... | collective-permute-start | bytes 786440 | tf_op jit(solution)/shard_map/ppermute | solution.py:20
  50.1 4.2 %collective-permute-start.11 = (bf16[8,256,512]{2,1,0:T(8,128)(2,1)S(1)}, bf16[8,256,512]{2,1,0:T(8,128)(2,1)S(1)}, u32[]{:S(2)}, u32[]{:S(2)}) collective-permute-start(bf16[8,256,512]{2,1,0:T(8,128)(2,1)S(1)} %stack_arrived.1.refs_2_.refs_6_), channel_id=1, source_target_pairs={{0,1},{1,0},{2,3},{3,2},{4,5},{5,4},{6,7},{7,6},{8,9},{9,8},{10,11... | collective-permute-start | bytes 6291464 | tf_op jit(solution)/shard_map/ppermute | solution.py:20
  68.1 4.4 %collective-permute-start.18 = (bf16[8,256,512]{2,1,0:T(8,128)(2,1)}, bf16[8,256,512]{2,1,0:T(8,128)(2,1)S(1)}, u32[]{:S(2)}, u32[]{:S(2)}) collective-permute-start(bf16[8,256,512]{2,1,0:T(8,128)(2,1)} %get-tuple-element.55), channel_id=1, source_target_pairs={{0,1},{1,0},{2,3},{3,2},{4,5},{5,4},{6,7},{7,6},{8,9},{9,8},{10,11... | collective-permute-start | bytes 6291464 | tf_op jit(solution)/shard_map/ppermute | solution.py:20
  75.3 13.4 %collective-permute-start.19 = (bf16[256,512]{1,0:T(8,128)(2,1)S(1)}, bf16[256,512]{1,0:T(8,128)(2,1)S(1)}, u32[]{:S(2)}, u32[]{:S(2)}) collective-permute-start(bf16[256,512]{1,0:T(8,128)(2,1)S(1)} %get-tuple-element.57), channel_id=1, source_target_pairs={{0,4},{1,5},{2,6},{3,7},{4,0},{5,1},{6,2},{7,3},{8,12},{9,13},{10,... | collective-permute-start | bytes 786440 | tf_op jit(solution)/shard_map/ppermute | solution.py:20
  75.4 13.3 %collective-permute-start.20 = (bf16[256,512]{1,0:T(8,128)(2,1)S(1)}, bf16[256,512]{1,0:T(8,128)(2,1)S(1)}, u32[]{:S(2)}, u32[]{:S(2)}) collective-permute-start(bf16[256,512]{1,0:T(8,128)(2,1)S(1)} %get-tuple-element.58), channel_id=1, source_target_pairs={{0,12},{1,13},{2,14},{3,15},{4,8},{5,9},{6,10},{7,11},{8,4},{9,5},... | collective-permute-start | bytes 786440 | tf_op jit(solution)/shard_map/ppermute | solution.py:20
  78.3 6.9 %collective-permute-start.14 = (f32[40,256]{1,0:T(8,128)S(1)}, f32[40,256]{1,0:T(8,128)S(1)}, u32[]{:S(2)}, u32[]{:S(2)}) collective-permute-start(f32[40,256]{1,0:T(8,128)S(1)} %copy-done.14), channel_id=1, source_target_pairs={{0,48},{16,32},{32,16},{48,0},{64,112},{80,96},{96,80},{112,64},{1... | collective-permute-start | bytes 122888 | tf_op jit(solution)/shard_map/ppermute | solution.py:20
  80.2 7.4 %collective-permute-start.13 = (f32[40,256]{1,0:T(8,128)S(1)}, f32[40,256]{1,0:T(8,128)S(1)}, u32[]{:S(2)}, u32[]{:S(2)}) collective-permute-start(f32[40,256]{1,0:T(8,128)S(1)} %copy-done.14), channel_id=1, source_target_pairs={{0,32},{16,48},{32,0},{48,16},{64,96},{80,112},{96,64},{112,80},{1... | collective-permute-start | bytes 122888 | tf_op jit(solution)/shard_map/ppermute | solution.py:20
  81.3 6.3 %collective-permute-start.12 = (f32[40,256]{1,0:T(8,128)S(1)}, f32[40,256]{1,0:T(8,128)S(1)}, u32[]{:S(2)}, u32[]{:S(2)}) collective-permute-start(f32[40,256]{1,0:T(8,128)S(1)} %copy-done.14), channel_id=1, source_target_pairs={{0,16},{16,0},{32,48},{48,32},{64,80},{80,64},{96,112},{112,96},{1... | collective-permute-start | bytes 122888 | tf_op jit(solution)/shard_map/ppermute | solution.py:20
  88.9 13.9 %collective-permute-start.21 = (bf16[2,256,512]{2,1,0:T(8,128)(2,1)S(1)}, bf16[2,256,512]{2,1,0:T(8,128)(2,1)S(1)}, u32[]{:S(2)}, u32[]{:S(2)}) collective-permute-start(bf16[2,256,512]{2,1,0:T(8,128)(2,1)S(1)} %get-tuple-element.59), channel_id=1, source_target_pairs={{0,4},{1,5},{2,6},{3,7},{4,0},{5,1},{6,2},{7,3},{8,12},{9,13},{10,... | collective-permute-start | bytes 1572872 | tf_op jit(solution)/shard_map/ppermute | solution.py:20
  90.3 12.9 %collective-permute-start.22 = (bf16[2,256,512]{2,1,0:T(8,128)(2,1)S(1)}, bf16[2,256,512]{2,1,0:T(8,128)(2,1)S(1)}, u32[]{:S(2)}, u32[]{:S(2)}) collective-permute-start(bf16[2,256,512]{2,1,0:T(8,128)(2,1)S(1)} %get-tuple-element.60), channel_id=1, source_target_pairs={{0,12},{1,13},{2,14},{3,15},{4,8},{5,9},{6,10},{7,11},{8,4},{9,5},... | collective-permute-start | bytes 1572872 | tf_op jit(solution)/shard_map/ppermute | solution.py:20
  90.9 9.8 %collective-permute-start.17 = (f32[40,256]{1,0:T(8,128)S(1)}, f32[40,256]{1,0:T(8,128)S(1)}, u32[]{:S(2)}, u32[]{:S(2)}) collective-permute-start(f32[40,256]{1,0:T(8,128)S(1)} %get-tuple-element.53.refs_0_.whole_ref), channel_id=1, source_target_pairs={{0,192},{16,208},{32,224},{48,240},{64,128},{80,144},{96,160},{112... | collective-permute-start | bytes 122888 | tf_op jit(solution)/shard_map/ppermute | solution.py:20
  92.9 7.8 %collective-permute-start.16 = (f32[40,256]{1,0:T(8,128)S(1)}, f32[40,256]{1,0:T(8,128)S(1)}, u32[]{:S(2)}, u32[]{:S(2)}) collective-permute-start(f32[40,256]{1,0:T(8,128)S(1)} %get-tuple-element.53.refs_0_.whole_ref), channel_id=1, source_target_pairs={{0,128},{16,144},{32,160},{48,176},{64,192},{80,208},{96,224},{112... | collective-permute-start | bytes 122888 | tf_op jit(solution)/shard_map/ppermute | solution.py:20
  93.7 9.1 %collective-permute-start.15 = (f32[40,256]{1,0:T(8,128)S(1)}, f32[40,256]{1,0:T(8,128)S(1)}, u32[]{:S(2)}, u32[]{:S(2)}) collective-permute-start(f32[40,256]{1,0:T(8,128)S(1)} %get-tuple-element.53.refs_0_.whole_ref), channel_id=1, source_target_pairs={{0,64},{16,80},{32,96},{48,112},{64,0},{80,16},{96,32},{112,48},{1... | collective-permute-start | bytes 122888 | tf_op jit(solution)/shard_map/ppermute | solution.py:20
  103.4 20.8 %collective-permute-start.23 = (bf16[256,512]{1,0:T(8,128)(2,1)S(1)}, bf16[256,512]{1,0:T(8,128)(2,1)S(1)}, u32[]{:S(2)}, u32[]{:S(2)}) collective-permute-start(bf16[256,512]{1,0:T(8,128)(2,1)S(1)} %get-tuple-element.62), channel_id=1, source_target_pairs={{0,2},{1,3},{2,0},{3,1},{4,6},{5,7},{6,4},{7,5},{8,10},{9,11},{10,... | collective-permute-start | bytes 786440 | tf_op jit(solution)/shard_map/ppermute | solution.py:20
  (24 other events, 158.9 us)
Sparse Core Ops, SparseCore 0:
  58.3 77.3 reduce-scatter.1
where the time goes:
time: 146 us; the launch traced here: 144 us
  waiting for transfers between devices  55.7 us (38%)
  starting transfers between devices  39.4 us (27%)
  Pallas kernels  17.9 us (12%)
  between operations  14.2 us (10%)
  local copies, waits for them, and re-layouts  13.8 us (9%)
  other arithmetic  3.24 us (2%)
    ppermute x24, waiting for transfers between devices, traded(): return lax.ppermute(value, axis, pairs)  45 us
    ppermute x24, starting transfers between devices, traded(): return lax.ppermute(value, axis, pairs)  39.4 us
    unnamed x46, local copies, waits for them, and re-layouts  13.8 us
    reduce_scatter x1, waiting for transfers between devices, on_device(): lax.psum_scatter(weight_share, 'ctx', scatter_dimension=1, tiled=True)  10.7 us
    pallas_call x11, Pallas kernels, ordered_call(): pl.pallas_call(skipping, in_specs=[ANY] * count + in_specs, **options)  10 us
    pallas_call x1, Pallas kernels, on_device(): pl.pallas_call(backward_local, grid=(tiles,), in_specs=[rows, rows, rows,...  3.1 us
  transfers between devices with their start and end apart: 25, of which 16 were waited for; matrix products, arithmetic and copies ran while one was open for 1% of the time, Pallas kernels for 11%

commit v1 on v0

--- a/solution.py
+++ b/solution.py
@@ -24,10 +24,21 @@
     return ref[pl.ds(offset + half * HALF * SUB, HALF, stride=SUB), :]
 
 
-def forward_local(key_ref, value_ref, rate_ref, weight_ref, skip_ref, state_ref, mixed_ref, product, carried, scaled):
+def shortfall(value):
+    series = jnp.ones_like(value)
+    for order in range(10, 1, -1):
+        series = 1.0 - value * (1.0 / order) * series
+    return jnp.where(value < 0.5, value * series, 1.0 - jnp.exp(-value))
+
+
+def forward_local(length, key_ref, value_ref, decay_ref, residue_ref, skip_ref, state_ref, mixed_ref, rate_ref, gain_ref, weight_ref, product, carried, scaled):
     product[...] = key_ref[...].astype(F32) * value_ref[...].astype(F32)
-    rates = rate_ref[...]
-    weights = weight_ref[...]
+    rates = decay_ref[...] * (1.0 / length)
+    gains = jnp.sqrt(shortfall(2.0 * rates) * (1.0 / rates.shape[0]))
+    weights = residue_ref[...] * gains
+    rate_ref[...] = rates
+    gain_ref[...] = gains
+    weight_ref[...] = weights
     pole = jnp.exp(-rates)
     leap = jnp.exp(-float(SUB) * rates)
     state = jnp.zeros_like(rates)
@@ -160,11 +171,10 @@
 
 def weight_part(position_ref, turned_ref, own_ref, other_ref, out_ref, token_ref):
     place = position_ref[0]
-    block = own_ref.shape[2]
     for ref, flip in ((own_ref, 0), (other_ref, 1)):
         for index, mask in enumerate(CHIP_MASKS):
-            first = pl.multiple_of((place ^ (mask | flip)) * block, block)
-            out_ref[:, pl.ds(first, block)] = jnp.dot(
+            target = place ^ (mask | flip)
+            out_ref[target & 7, lax.shift_right_logical(target, 3)] = jnp.dot(
                 turned_ref[...], ref[index], preferred_element_type=F32
             ).astype(BF16)
     token_ref[...] = jnp.zeros(token_ref.shape, F32)
@@ -286,6 +296,11 @@
         ref[...] = total.astype(ref.dtype)
 
 
+def join_weight(position_ref, kept_ref, arrived_ref, out_ref):
+    side = lax.shift_right_logical(position_ref[1], 3)
+    out_ref[...] = kept_ref[side].astype(F32) + widened(arrived_ref)
+
+
 def merge_last(kept_ref, arrived_ref, out_ref):
     out_ref[...] = (kept_ref[...] + widened(arrived_ref)).astype(BF16)
 
@@ -344,9 +359,6 @@
     ctx_count = lax.axis_size("ctx")
     chan_count = lax.axis_size("chan")
     positions = jnp.stack([lax.axis_index("chan"), lax.axis_index("ctx")]).astype(jnp.int32)
-    rates = decays / (tokens * ctx_count)
-    gains = jnp.sqrt(-jnp.expm1(-2.0 * rates) / modes)
-    weights = residues * gains
     skip_row = skip_gain.reshape(1, width)
     tiles = width // LANES
     rows = tile_of(tokens)
@@ -364,15 +376,15 @@
     tall_shape = shape_of(tall, width)
 
     arrived = traded(cotangent, "chan", 2)
-    state, local = pl.pallas_call(
-        forward_local,
+    state, local, rates, gains, weights = pl.pallas_call(
+        functools.partial(forward_local, tokens * ctx_count),
         grid=(tiles,),
         in_specs=[rows, rows, few, few, one],
-        out_specs=[few, rows],
-        out_shape=[state_shape, square],
+        out_specs=[few, rows, few, few, few],
+        out_shape=[state_shape, square, state_shape, state_shape, state_shape],
         scratch_shapes=[block_scratch] * 3,
         name="forward_local",
-    )(key_rows, value_rows, rates, weights, skip_row)
+    )(key_rows, value_rows, decays, residues, skip_row)
     near = [state] + [traded(state, "ctx", mask) for mask in (1, 2, 3)]
     inside, whole, pair = local_call(
         functools.partial(forward_near, tokens),
@@ -409,14 +421,20 @@
     sibling = traded(own, "chan", 1)
     weight_share, token = local_call(
         weight_part,
-        [kind_of(width, chan_count * columns), shape_of(HALF, LANES)],
+        [kind_of(8, 2, width, columns), shape_of(HALF, LANES)],
         positions,
         gated_turned,
         own,
         sibling,
         scalars=1,
     )
-    weight_grad = lax.psum_scatter(weight_share, "ctx", scatter_dimension=1, tiled=True)
+    weight_grad = lax.psum_scatter(
+        weight_share,
+        "ctx",
+        scatter_dimension=0,
+        axis_index_groups=[list(range(8)), list(range(8, 16))],
+        tiled=False,
+    )
     query_grad, drive, other, mine = local_call(
         project_rows,
         [kind_of(tokens, width), square, eight, eight],
@@ -493,6 +511,20 @@
         scratch_shapes=[block_scratch] * 2,
         name="backward_mix",
     )(positions, back_local, key_rows, value_rows, rates, weights, inside, whole, *across)
+    side = lax.axis_index("ctx") >> 3
+    whole_of = lambda *shape: pl.BlockSpec(shape, lambda step: (0,) * len(shape))
+    weight_grad = pl.pallas_call(
+        join_weight,
+        grid=(1,),
+        in_specs=[SMEM, whole_of(2, width, columns), whole_of(width, columns)],
+        out_specs=whole_of(width, columns),
+        out_shape=shape_of(width, columns),
+        name="join_weight",
+    )(
+        positions,
+        weight_grad,
+        traded(lax.dynamic_index_in_dim(weight_grad, 1 - side, 0, keepdims=False), "ctx", 8),
+    )
     return (
         layer_out,
         query_grad,
@@ -500,7 +532,7 @@
         value_grad,
         residue_grad,
         skip_sum.reshape(width),
-        weight_grad.astype(F32),
+        weight_grad,
     )
 
 

time: 146 us -> 133 us (0.911)
  waiting for transfers between devices: 55.7 us -> 38.5 us
  local copies, waits for them, and re-layouts: 13.8 us -> 17.9 us
  Pallas kernels: 17.9 us -> 21.5 us
  other arithmetic: 3.24 us -> 0.07 us
    ppermute x24 -> x25, waiting for transfers between devices: 45 us -> 34.2 us  [traded(): return lax.ppermute(value, axis, pairs)]
    reduce_scatter x1, waiting for transfers between devices: 10.7 us -> 4.29 us  [on_device(): lax.psum_scatter(weight_share, 'ctx', scatter_dimension=0, axis_index_gro...]
    unnamed x46 -> x54, local copies, waits for them, and re-layouts: 13.8 us -> 16.9 us
    pallas_call x1 -> x2, Pallas kernels: 2.51 us -> 4.5 us  [the longest x1 2.53 us: on_device(): pl.pallas_call(functools.partial(forward_local, tokens * ctx_count), grid...]
    convert_element_type x1 -> x0, other arithmetic: 1.8 us -> none  [on_device(): weight_grad.astype(F32)]
    pallas_call x11, Pallas kernels: 10 us -> 11.6 us  [ordered_call(): pl.pallas_call(skipping, in_specs=[ANY] * count + in_specs, **options)]
    ppermute x24 -> x25, starting transfers between devices: 39.4 us -> 39.3 us  [traded(): return lax.ppermute(value, axis, pairs)]
  transfers between devices with their start and end apart: 25 -> 26, of which waited for: 16 -> 16; matrix products, arithmetic and copies ran while one was open for 1% -> 1% of each run, Pallas kernels for 11% -> 13%
where the time goes in v1:
time: 133 us; the launch traced here: 132 us
  starting transfers between devices  39.4 us (30%)
  waiting for transfers between devices  38.5 us (29%)
  Pallas kernels  21.5 us (16%)
  local copies, waits for them, and re-layouts  17.9 us (13%)
  between operations  14.2 us (11%)
    ppermute x25, starting transfers between devices, traded(): return lax.ppermute(value, axis, pairs)  39.3 us
    ppermute x25, waiting for transfers between devices, traded(): return lax.ppermute(value, axis, pairs)  34.2 us
    unnamed x54, local copies, waits for them, and re-layouts  16.9 us
    pallas_call x11, Pallas kernels, ordered_call(): pl.pallas_call(skipping, in_specs=[ANY] * count + in_specs, **options)  11.6 us
    reduce_scatter x1, waiting for transfers between devices, on_device(): lax.psum_scatter(weight_share, 'ctx', scatter_dimension=0, axis_index_gro...  4.29 us
    pallas_call x1, Pallas kernels, on_device(): pl.pallas_call(backward_local, grid=(tiles,), in_specs=[rows, rows, rows,...  3.1 us
  transfers between devices with their start and end apart: 26, of which 16 were waited for; matrix products, arithmetic and copies ran while one was open for 1% of the time, Pallas kernels for 13%

profile of v1, /device:TPU:14, one launch (start us, length us, event | category | flops | bytes accessed | tf_op | source)
XLA Modules:
  0.0 131.6 jit_solution(5434729493910861535)
XLA Ops:
  7.2 2.4 %collective-permute-start.3 = (bf16[256,512]{1,0:T(8,128)(2,1)}, bf16[256,512]{1,0:T(8,128)(2,1)S(1)}, u32[]{:S(2)}, u32[]{:S(2)}) collective-permute-start(bf16[256,512]{1,0:T(8,128)(2,1)} %refs_6_.1), channel_id=1, source_target_pairs={{0,2},{1,3},{2,0},{3,1},{4,6},{5,7},{6,4},{7,5},{8,10},{9,11},{10,... | collective-permute-start | bytes 786440 | tf_op jit(solution)/shard_map/ppermute | solution.py:20
  9.6 2.5 %forward_local.1 = (f32[16,256]{1,0:T(8,128)}, f32[256,256]{1,0:T(8,128)}, f32[16,256]{1,0:T(8,128)}, f32[16,256]{1,0:T(8,128)}, f32[16,256]{1,0:T(8,128)}) custom-call(bf16[256,256]{1,0:T(8,128)(2,1)} %key_ref.5, bf16[256,256]{1,0:T(8,128)(2,1)} %value_ref.5, f32[16,256]{1,0:T(8,128)} %decay_ref.1, f32[16,256]{1,0:T(8,128)} %residue_ref.1, f32[1,256]{1,0:T(1,128)} %bitcast.8), custom_call_target="tpu_custom_call" | custom-call | tf_op jit(solution)/shard_map/forward_local/pallas_call | solution.py:379
  12.1 4.7 %collective-permute-start.2 = (f32[16,256]{1,0:T(8,128)}, f32[16,256]{1,0:T(8,128)S(1)}, u32[]{:S(2)}, u32[]{:S(2)}) collective-permute-start(f32[16,256]{1,0:T(8,128)} %get-tuple-element.43.refs_2_), channel_id=1, source_target_pairs={{0,48},{16,32},{32,16},{48,0},{64,112},{80,96},{96,80},{112,64},{1... | collective-permute-start | bytes 49160 | tf_op jit(solution)/shard_map/ppermute | solution.py:20
  18.8 2.9 %collective-permute-done.1.refs_4_ = f32[16,256]{1,0:T(8,128)S(1)} collective-permute-done((f32[16,256]{1,0:T(8,128)}, f32[16,256]{1,0:T(8,128)S(1)}, u32[]{:S(2)}, u32[]{:S(2)}) %collective-permute-start.1) | collective-permute-done | bytes 16416 | tf_op jit(solution)/shard_map/ppermute | solution.py:20
  26.1 5.3 %collective-permute-start.6 = (f32[16,256]{1,0:T(8,128)S(1)}, f32[16,256]{1,0:T(8,128)S(1)}, u32[]{:S(2)}, u32[]{:S(2)}) collective-permute-start(f32[16,256]{1,0:T(8,128)S(1)} %get-tuple-element.44), channel_id=1, source_target_pairs={{0,192},{16,208},{32,224},{48,240},{64,128},{80,144},{96,160},{112... | collective-permute-start | bytes 49160 | tf_op jit(solution)/shard_map/ppermute | solution.py:20
  35.1 4.6 %collective-permute-done.4.refs_0_.refs_7_ = f32[16,256]{1,0:T(8,128)S(1)} collective-permute-done((f32[16,256]{1,0:T(8,128)S(1)}, f32[16,256]{1,0:T(8,128)S(1)}, u32[]{:S(2)}, u32[]{:S(2)}) %collective-permute-start.4) | collective-permute-done | bytes 16416 | tf_op jit(solution)/shard_map/ppermute | solution.py:20
  41.0 2.8 %collective-permute-start.9 = (bf16[256,512]{1,0:T(8,128)(2,1)S(1)}, bf16[256,512]{1,0:T(8,128)(2,1)S(1)}, u32[]{:S(2)}, u32[]{:S(2)}) collective-permute-start(bf16[256,512]{1,0:T(8,128)(2,1)S(1)} %get-tuple-element.46.refs_0_), channel_id=1, source_target_pairs={{0,12},{1,13},{2,14},{3,15},{4,8},{5,9},{6,10},{7,11},{8,4},{9,5},... | collective-permute-start | bytes 786440 | tf_op jit(solution)/shard_map/ppermute | solution.py:20
  43.9 2.4 %collective-permute-done.10.refs_4_ = bf16[256,512]{1,0:T(8,128)(2,1)S(1)} collective-permute-done((bf16[256,512]{1,0:T(8,128)(2,1)S(1)}, bf16[256,512]{1,0:T(8,128)(2,1)S(1)}, u32[]{:S(2)}, u32[]{:S(2)}) %collective-permute-start.10) | collective-permute-done | bytes 262176 | tf_op jit(solution)/shard_map/ppermute | solution.py:20
  46.2 2.4 %collective-permute-done.9.refs_3_ = bf16[256,512]{1,0:T(8,128)(2,1)S(1)} collective-permute-done((bf16[256,512]{1,0:T(8,128)(2,1)S(1)}, bf16[256,512]{1,0:T(8,128)(2,1)S(1)}, u32[]{:S(2)}, u32[]{:S(2)}) %collective-permute-start.9) | collective-permute-done | bytes 262176 | tf_op jit(solution)/shard_map/ppermute | solution.py:20
  50.2 2.8 %collective-permute-done.11.refs_3_.refs_7_ = bf16[8,256,512]{2,1,0:T(8,128)(2,1)S(1)} collective-permute-done((bf16[8,256,512]{2,1,0:T(8,128)(2,1)S(1)}, bf16[8,256,512]{2,1,0:T(8,128)(2,1)S(1)}, u32[]{:S(2)}, u32[]{:S(2)}) %collective-permute-start.11) | collective-permute-done | bytes 2097184 | tf_op jit(solution)/shard_map/ppermute | solution.py:20
  54.9 2.0 %copy-done.3 = bf16[8,2,256,512]{3,2,1,0:T(8,128)(2,1)} copy-done((bf16[8,2,256,512]{3,2,1,0:T(8,128)(2,1)}, bf16[8,2,256,512]{3,2,1,0:T(8,128)(2,1)S(1)}, u32[]{:S(2)}) %copy-start.3) | copy-done | bytes 4194328
  58.5 2.2 %copy-done.2 = bf16[256,8192]{1,0:T(8,128)(2,1)S(1)} copy-done((bf16[256,8192]{1,0:T(8,128)(2,1)S(1)}, bf16[256,8192]{1,0:T(8,128)(2,1)}, u32[]{:S(2)}) %copy-start.2) | copy-done | bytes 4194328
  60.7 4.1 %project_rows.1 = (bf16[256,256]{1,0:T(8,128)(2,1)}, f32[256,256]{1,0:T(8,128)S(1)}, bf16[8,256,512]{2,1,0:T(8,128)(2,1)}, bf16[8,256,512]{2,1,0:T(8,128)(2,1)S(1)}) custom-call(f32[8,128]{1,0:T(8,128)S(1)} %get-tuple-element.52.refs_0_, s32[2]{0:T(128)S(1)} %pad_add_fusion.refs_0_.refs_1_.position_ref, bf16[256,256]{1,0:T(8,128)(2,1)S(1)} %copy-done.8, ...), custom_call_target="tpu_custom_call" | custom-call | tf_op jit(solution)/shard_map/project_rows/pallas_call | solution.py:327
  67.0 3.1 %backward_local.1 = (f32[256,256]{1,0:T(8,128)}, f32[40,256]{1,0:T(8,128)}) custom-call(f32[256,256]{1,0:T(8,128)} %copy-done.14, bf16[256,256]{1,0:T(8,128)(2,1)} %key_ref.5, bf16[256,256]{1,0:T(8,128)(2,1)} %value_ref.5, f32[16,256]{1,0:T(8,128)} %get-tuple-element.42.refs_1_.refs_4_.rate_ref, f32[16,256]{1,0:T(8,128)} %get-tuple-element.48.refs_5_.weight_ref, ...), custom_call_target="tpu_custom_call" | custom-call | tf_op jit(solution)/shard_map/backward_local/pallas_call | solution.py:452
  77.2 2.8 %collective-permute-start.20 = (bf16[256,512]{1,0:T(8,128)(2,1)S(1)}, bf16[256,512]{1,0:T(8,128)(2,1)S(1)}, u32[]{:S(2)}, u32[]{:S(2)}) collective-permute-start(bf16[256,512]{1,0:T(8,128)(2,1)S(1)} %get-tuple-element.64), channel_id=1, source_target_pairs={{0,12},{1,13},{2,14},{3,15},{4,8},{5,9},{6,10},{7,11},{8,4},{9,5},... | collective-permute-start | bytes 786440 | tf_op jit(solution)/shard_map/ppermute | solution.py:20
  84.4 2.7 %collective-permute-done.14.refs_5_ = f32[40,256]{1,0:T(8,128)S(1)} collective-permute-done((f32[40,256]{1,0:T(8,128)S(1)}, f32[40,256]{1,0:T(8,128)S(1)}, u32[]{:S(2)}, u32[]{:S(2)}) %collective-permute-start.14) | collective-permute-done | bytes 40992 | tf_op jit(solution)/shard_map/ppermute | solution.py:20
  87.1 2.3 %collective-permute-done.13.refs_4_ = f32[40,256]{1,0:T(8,128)S(1)} collective-permute-done((f32[40,256]{1,0:T(8,128)S(1)}, f32[40,256]{1,0:T(8,128)S(1)}, u32[]{:S(2)}, u32[]{:S(2)}) %collective-permute-start.13) | collective-permute-done | bytes 40992 | tf_op jit(solution)/shard_map/ppermute | solution.py:20
  93.7 2.2 %collective-permute-start.17 = (f32[40,256]{1,0:T(8,128)S(1)}, f32[40,256]{1,0:T(8,128)S(1)}, u32[]{:S(2)}, u32[]{:S(2)}) collective-permute-start(f32[40,256]{1,0:T(8,128)S(1)} %get-tuple-element.59.refs_0_.whole_ref), channel_id=1, source_target_pairs={{0,192},{16,208},{32,224},{48,240},{64,128},{80,144},{96,160},{112... | collective-permute-start | bytes 122888 | tf_op jit(solution)/shard_map/ppermute | solution.py:20
  96.5 4.6 %collective-permute-start.15 = (f32[40,256]{1,0:T(8,128)S(1)}, f32[40,256]{1,0:T(8,128)S(1)}, u32[]{:S(2)}, u32[]{:S(2)}) collective-permute-start(f32[40,256]{1,0:T(8,128)S(1)} %get-tuple-element.59.refs_0_.whole_ref), channel_id=1, source_target_pairs={{0,64},{16,80},{32,96},{48,112},{64,0},{80,16},{96,32},{112,48},{1... | collective-permute-start | bytes 122888 | tf_op jit(solution)/shard_map/ppermute | solution.py:20
  101.1 3.2 %collective-permute-done.17.refs_2_.third_ref = f32[40,256]{1,0:T(8,128)S(1)} collective-permute-done((f32[40,256]{1,0:T(8,128)S(1)}, f32[40,256]{1,0:T(8,128)S(1)}, u32[]{:S(2)}, u32[]{:S(2)}) %collective-permute-start.17) | collective-permute-done | bytes 40992 | tf_op jit(solution)/shard_map/ppermute | solution.py:20
  108.9 4.3 %reduce-scatter.2.cloned.1.call-done = bf16[1,2,256,512]{3,2,1,0:T(8,128)(2,1)} async-done(((bf16[8,2,256,512]{3,2,1,0:T(8,128)(2,1)}), bf16[1,2,256,512]{3,2,1,0:T(8,128)(2,1)}) %reduce-scatter.2.cloned.1.call-update) | async-done | bytes 524304 | tf_op jit(solution)/shard_map/reduce_scatter | solution.py:431
  114.8 2.2 %backward_mix.1 = (bf16[256,256]{1,0:T(8,128)(2,1)}, bf16[256,256]{1,0:T(8,128)(2,1)}, f32[16,256]{1,0:T(8,128)}, f32[1,256]{1,0:T(1,128)}) custom-call(s32[2]{0:T(128)} %copy-done.22, f32[256,256]{1,0:T(8,128)} %get-tuple-element.70.local_ref, bf16[256,256]{1,0:T(8,128)(2,1)} %key_ref.5, bf16[256,256]{1,0:T(8,128)(2,1)} %value_ref.5, ...), custom_call_target="tpu_custom_call" | custom-call | tf_op jit(solution)/shard_map/backward_mix/pallas_call | solution.py:500
  117.8 4.2 %collective-permute-done.24.arrived_ref = bf16[256,512]{1,0:T(8,128)(2,1)S(1)} collective-permute-done((bf16[256,512]{1,0:T(8,128)(2,1)S(1)}, bf16[256,512]{1,0:T(8,128)(2,1)S(1)}, u32[]{:S(2)}, u32[]{:S(2)}) %collective-permute-start.24) | collective-permute-done | bytes 262176 | tf_op jit(solution)/shard_map/ppermute | solution.py:20
  122.7 2.0 %join_weight.1 = f32[256,512]{1,0:T(8,128)} custom-call(s32[2]{0:T(128)} %copy-done.22, bf16[2,256,512]{2,1,0:T(8,128)(2,1)} %bitcast.7, bf16[256,512]{1,0:T(8,128)(2,1)} %copy-done.26), custom_call_target="tpu_custom_call" | custom-call | tf_op jit(solution)/shard_map/join_weight/pallas_call | solution.py:516
  (100 shorter events, 42.5 us)
Async XLA Ops:
  7.2 106.0 %reduce-scatter.2.cloned.1.call-start = ((), (), s32[]{:S(2)}) async-start(), calls=%async_computation.1 | async-start | bytes 4718592 | tf_op jit(solution)/shard_map/reduce_scatter | solution.py:431
  7.2 14.5 %collective-permute-start.3 = (bf16[256,512]{1,0:T(8,128)(2,1)}, bf16[256,512]{1,0:T(8,128)(2,1)S(1)}, u32[]{:S(2)}, u32[]{:S(2)}) collective-permute-start(bf16[256,512]{1,0:T(8,128)(2,1)} %refs_6_.1), channel_id=1, source_target_pairs={{0,2},{1,3},{2,0},{3,1},{4,6},{5,7},{6,4},{7,5},{8,10},{9,11},{10,... | collective-permute-start | bytes 786440 | tf_op jit(solution)/shard_map/ppermute | solution.py:20
  12.1 6.7 %collective-permute-start.2 = (f32[16,256]{1,0:T(8,128)}, f32[16,256]{1,0:T(8,128)S(1)}, u32[]{:S(2)}, u32[]{:S(2)}) collective-permute-start(f32[16,256]{1,0:T(8,128)} %get-tuple-element.43.refs_2_), channel_id=1, source_target_pairs={{0,48},{16,32},{32,16},{48,0},{64,112},{80,96},{96,80},{112,64},{1... | collective-permute-start | bytes 49160 | tf_op jit(solution)/shard_map/ppermute | solution.py:20
  16.8 4.8 %collective-permute-start.1 = (f32[16,256]{1,0:T(8,128)}, f32[16,256]{1,0:T(8,128)S(1)}, u32[]{:S(2)}, u32[]{:S(2)}) collective-permute-start(f32[16,256]{1,0:T(8,128)} %get-tuple-element.43.refs_2_), channel_id=1, source_target_pairs={{0,32},{16,48},{32,0},{48,16},{64,96},{80,112},{96,64},{112,80},{1... | collective-permute-start | bytes 49160 | tf_op jit(solution)/shard_map/ppermute | solution.py:20
  16.8 4.8 %collective-permute-start = (f32[16,256]{1,0:T(8,128)}, f32[16,256]{1,0:T(8,128)S(1)}, u32[]{:S(2)}, u32[]{:S(2)}) collective-permute-start(f32[16,256]{1,0:T(8,128)} %get-tuple-element.43.refs_2_), channel_id=1, source_target_pairs={{0,16},{16,0},{32,48},{48,32},{64,80},{80,64},{96,112},{112,96},{1... | collective-permute-start | bytes 49160 | tf_op jit(solution)/shard_map/ppermute | solution.py:20
  24.7 15.1 %collective-permute-start.8 = (bf16[2,256,512]{2,1,0:T(8,128)(2,1)S(1)}, bf16[2,256,512]{2,1,0:T(8,128)(2,1)S(1)}, u32[]{:S(2)}, u32[]{:S(2)}) collective-permute-start(bf16[2,256,512]{2,1,0:T(8,128)(2,1)S(1)} %get-tuple-element.45.refs_0_), channel_id=1, source_target_pairs={{0,12},{1,13},{2,14},{3,15},{4,8},{5,9},{6,10},{7,11},{8,4},{9,5},... | collective-permute-start | bytes 1572872 | tf_op jit(solution)/shard_map/ppermute | solution.py:20
  25.2 14.5 %collective-permute-start.7 = (bf16[2,256,512]{2,1,0:T(8,128)(2,1)S(1)}, bf16[2,256,512]{2,1,0:T(8,128)(2,1)S(1)}, u32[]{:S(2)}, u32[]{:S(2)}) collective-permute-start(bf16[2,256,512]{2,1,0:T(8,128)(2,1)S(1)} %get-tuple-element.45.refs_0_), channel_id=1, source_target_pairs={{0,4},{1,5},{2,6},{3,7},{4,0},{5,1},{6,2},{7,3},{8,12},{9,13},{10,... | collective-permute-start | bytes 1572872 | tf_op jit(solution)/shard_map/ppermute | solution.py:20
  26.1 8.7 %collective-permute-start.6 = (f32[16,256]{1,0:T(8,128)S(1)}, f32[16,256]{1,0:T(8,128)S(1)}, u32[]{:S(2)}, u32[]{:S(2)}) collective-permute-start(f32[16,256]{1,0:T(8,128)S(1)} %get-tuple-element.44), channel_id=1, source_target_pairs={{0,192},{16,208},{32,224},{48,240},{64,128},{80,144},{96,160},{112... | collective-permute-start | bytes 49160 | tf_op jit(solution)/shard_map/ppermute | solution.py:20
  32.1 7.6 %collective-permute-start.4 = (f32[16,256]{1,0:T(8,128)S(1)}, f32[16,256]{1,0:T(8,128)S(1)}, u32[]{:S(2)}, u32[]{:S(2)}) collective-permute-start(f32[16,256]{1,0:T(8,128)S(1)} %get-tuple-element.44), channel_id=1, source_target_pairs={{0,64},{16,80},{32,96},{48,112},{64,0},{80,16},{96,32},{112,48},{1... | collective-permute-start | bytes 49160 | tf_op jit(solution)/shard_map/ppermute | solution.py:20
  39.8 6.5 %collective-permute-start.10 = (bf16[256,512]{1,0:T(8,128)(2,1)S(1)}, bf16[256,512]{1,0:T(8,128)(2,1)S(1)}, u32[]{:S(2)}, u32[]{:S(2)}) collective-permute-start(bf16[256,512]{1,0:T(8,128)(2,1)S(1)} %get-tuple-element.51), channel_id=1, source_target_pairs={{0,4},{1,5},{2,6},{3,7},{4,0},{5,1},{6,2},{7,3},{8,12},{9,13},{10,... | collective-permute-start | bytes 786440 | tf_op jit(solution)/shard_map/ppermute | solution.py:20
  41.0 7.7 %collective-permute-start.9 = (bf16[256,512]{1,0:T(8,128)(2,1)S(1)}, bf16[256,512]{1,0:T(8,128)(2,1)S(1)}, u32[]{:S(2)}, u32[]{:S(2)}) collective-permute-start(bf16[256,512]{1,0:T(8,128)(2,1)S(1)} %get-tuple-element.46.refs_0_), channel_id=1, source_target_pairs={{0,12},{1,13},{2,14},{3,15},{4,8},{5,9},{6,10},{7,11},{8,4},{9,5},... | collective-permute-start | bytes 786440 | tf_op jit(solution)/shard_map/ppermute | solution.py:20
  66.8 4.4 %collective-permute-start.18 = (bf16[8,256,512]{2,1,0:T(8,128)(2,1)}, bf16[8,256,512]{2,1,0:T(8,128)(2,1)S(1)}, u32[]{:S(2)}, u32[]{:S(2)}) collective-permute-start(bf16[8,256,512]{2,1,0:T(8,128)(2,1)} %get-tuple-element.61), channel_id=1, source_target_pairs={{0,1},{1,0},{2,3},{3,2},{4,5},{5,4},{6,7},{7,6},{8,9},{9,8},{10,11... | collective-permute-start | bytes 6291464 | tf_op jit(solution)/shard_map/ppermute | solution.py:20
  77.1 13.6 %collective-permute-start.19 = (bf16[256,512]{1,0:T(8,128)(2,1)S(1)}, bf16[256,512]{1,0:T(8,128)(2,1)S(1)}, u32[]{:S(2)}, u32[]{:S(2)}) collective-permute-start(bf16[256,512]{1,0:T(8,128)(2,1)S(1)} %get-tuple-element.63), channel_id=1, source_target_pairs={{0,4},{1,5},{2,6},{3,7},{4,0},{5,1},{6,2},{7,3},{8,12},{9,13},{10,... | collective-permute-start | bytes 786440 | tf_op jit(solution)/shard_map/ppermute | solution.py:20
  77.2 13.5 %collective-permute-start.20 = (bf16[256,512]{1,0:T(8,128)(2,1)S(1)}, bf16[256,512]{1,0:T(8,128)(2,1)S(1)}, u32[]{:S(2)}, u32[]{:S(2)}) collective-permute-start(bf16[256,512]{1,0:T(8,128)(2,1)S(1)} %get-tuple-element.64), channel_id=1, source_target_pairs={{0,12},{1,13},{2,14},{3,15},{4,8},{5,9},{6,10},{7,11},{8,4},{9,5},... | collective-permute-start | bytes 786440 | tf_op jit(solution)/shard_map/ppermute | solution.py:20
  80.0 7.1 %collective-permute-start.14 = (f32[40,256]{1,0:T(8,128)S(1)}, f32[40,256]{1,0:T(8,128)S(1)}, u32[]{:S(2)}, u32[]{:S(2)}) collective-permute-start(f32[40,256]{1,0:T(8,128)S(1)} %copy-done.16), channel_id=1, source_target_pairs={{0,48},{16,32},{32,16},{48,0},{64,112},{80,96},{96,80},{112,64},{1... | collective-permute-start | bytes 122888 | tf_op jit(solution)/shard_map/ppermute | solution.py:20
  81.9 7.5 %collective-permute-start.13 = (f32[40,256]{1,0:T(8,128)S(1)}, f32[40,256]{1,0:T(8,128)S(1)}, u32[]{:S(2)}, u32[]{:S(2)}) collective-permute-start(f32[40,256]{1,0:T(8,128)S(1)} %copy-done.16), channel_id=1, source_target_pairs={{0,32},{16,48},{32,0},{48,16},{64,96},{80,112},{96,64},{112,80},{1... | collective-permute-start | bytes 122888 | tf_op jit(solution)/shard_map/ppermute | solution.py:20
  83.0 6.4 %collective-permute-start.12 = (f32[40,256]{1,0:T(8,128)S(1)}, f32[40,256]{1,0:T(8,128)S(1)}, u32[]{:S(2)}, u32[]{:S(2)}) collective-permute-start(f32[40,256]{1,0:T(8,128)S(1)} %copy-done.16), channel_id=1, source_target_pairs={{0,16},{16,0},{32,48},{48,32},{64,80},{80,64},{96,112},{112,96},{1... | collective-permute-start | bytes 122888 | tf_op jit(solution)/shard_map/ppermute | solution.py:20
  91.8 14.1 %collective-permute-start.21 = (bf16[2,256,512]{2,1,0:T(8,128)(2,1)}, bf16[2,256,512]{2,1,0:T(8,128)(2,1)S(1)}, u32[]{:S(2)}, u32[]{:S(2)}) collective-permute-start(bf16[2,256,512]{2,1,0:T(8,128)(2,1)} %get-tuple-element.65), channel_id=1, source_target_pairs={{0,4},{1,5},{2,6},{3,7},{4,0},{5,1},{6,2},{7,3},{8,12},{9,13},{10,... | collective-permute-start | bytes 1572872 | tf_op jit(solution)/shard_map/ppermute | solution.py:20
  92.9 14.0 %collective-permute-start.22 = (bf16[2,256,512]{2,1,0:T(8,128)(2,1)}, bf16[2,256,512]{2,1,0:T(8,128)(2,1)S(1)}, u32[]{:S(2)}, u32[]{:S(2)}) collective-permute-start(bf16[2,256,512]{2,1,0:T(8,128)(2,1)} %get-tuple-element.66), channel_id=1, source_target_pairs={{0,12},{1,13},{2,14},{3,15},{4,8},{5,9},{6,10},{7,11},{8,4},{9,5},... | collective-permute-start | bytes 1572872 | tf_op jit(solution)/shard_map/ppermute | solution.py:20
  93.7 10.6 %collective-permute-start.17 = (f32[40,256]{1,0:T(8,128)S(1)}, f32[40,256]{1,0:T(8,128)S(1)}, u32[]{:S(2)}, u32[]{:S(2)}) collective-permute-start(f32[40,256]{1,0:T(8,128)S(1)} %get-tuple-element.59.refs_0_.whole_ref), channel_id=1, source_target_pairs={{0,192},{16,208},{32,224},{48,240},{64,128},{80,144},{96,160},{112... | collective-permute-start | bytes 122888 | tf_op jit(solution)/shard_map/ppermute | solution.py:20
  95.9 8.4 %collective-permute-start.16 = (f32[40,256]{1,0:T(8,128)S(1)}, f32[40,256]{1,0:T(8,128)S(1)}, u32[]{:S(2)}, u32[]{:S(2)}) collective-permute-start(f32[40,256]{1,0:T(8,128)S(1)} %get-tuple-element.59.refs_0_.whole_ref), channel_id=1, source_target_pairs={{0,128},{16,144},{32,160},{48,176},{64,192},{80,208},{96,224},{112... | collective-permute-start | bytes 122888 | tf_op jit(solution)/shard_map/ppermute | solution.py:20
  96.5 9.4 %collective-permute-start.15 = (f32[40,256]{1,0:T(8,128)S(1)}, f32[40,256]{1,0:T(8,128)S(1)}, u32[]{:S(2)}, u32[]{:S(2)}) collective-permute-start(f32[40,256]{1,0:T(8,128)S(1)} %get-tuple-element.59.refs_0_.whole_ref), channel_id=1, source_target_pairs={{0,64},{16,80},{32,96},{48,112},{64,0},{80,16},{96,32},{112,48},{1... | collective-permute-start | bytes 122888 | tf_op jit(solution)/shard_map/ppermute | solution.py:20
  107.7 9.3 %collective-permute-start.23 = (bf16[256,512]{1,0:T(8,128)(2,1)}, bf16[256,512]{1,0:T(8,128)(2,1)S(1)}, u32[]{:S(2)}, u32[]{:S(2)}) collective-permute-start(bf16[256,512]{1,0:T(8,128)(2,1)} %get-tuple-element.68), channel_id=1, source_target_pairs={{0,2},{1,3},{2,0},{3,1},{4,6},{5,7},{6,4},{7,5},{8,10},{9,11},{10,... | collective-permute-start | bytes 786440 | tf_op jit(solution)/shard_map/ppermute | solution.py:20
  114.2 7.9 %collective-permute-start.24 = (bf16[256,512]{1,0:T(8,128)(2,1)S(1)}, bf16[256,512]{1,0:T(8,128)(2,1)S(1)}, u32[]{:S(2)}, u32[]{:S(2)}) collective-permute-start(bf16[256,512]{1,0:T(8,128)(2,1)S(1)} %dynamic-slice_bitcast_fusion), channel_id=1, source_target_pairs={{0,128},{16,144},{32,160},{48,176},{64,192},{80,208},{96,224},{112... | collective-permute-start | bytes 786440 | tf_op jit(solution)/shard_map/ppermute | solution.py:20
  (29 other events, 198.2 us)
Sparse Core Ops, SparseCore 0:
  57.0 56.1 reduce-scatter.1

commit v2 on v1

--- a/solution.py
+++ b/solution.py
@@ -48,7 +48,8 @@
         for step in range(1, SUB):
             inner = pole * inner + product[pl.ds(block * SUB + step, 1), :]
         state = leap * state + inner
-    state_ref[...] = state
+    state_ref[pl.ds(0, SUB), :] = state
+    state_ref[pl.ds(SUB, SUB), :] = rates
     taps = []
     power = weights
     for step in range(SUB):
@@ -80,9 +81,7 @@
     return jnp.exp(-reach * rates) * present
 
 
-def near_sums(backward, tokens, position_ref, rate_ref, value_refs, inside_ref, whole_ref):
-    values = [ref[...] for ref in value_refs]
-    rates = rate_ref[...]
+def near_sums(backward, tokens, position_ref, rates, values, inside_ref, whole_ref):
     modes = rates.shape[0]
     low = position_ref[1] & 3
     inside = jnp.zeros_like(rates)
@@ -96,14 +95,16 @@
         whole = whole + falling(rates, tokens * far) * state
     inside_ref[...] = inside
     whole_ref[pl.ds(0, modes), :] = whole
-    if values[0].shape[0] > modes:
+    if backward:
         sums = [value[modes:] for value in values]
         whole_ref[pl.ds(modes, sums[0].shape[0]), :] = (sums[0] + sums[1]) + (sums[2] + sums[3])
 
 
-def forward_near(tokens, position_ref, rate_ref, *rest):
+def forward_near(tokens, position_ref, *rest):
     own_ref, arrived_ref, inside_ref, whole_ref, pair_ref = rest[4:]
-    near_sums(False, tokens, position_ref, rate_ref, rest[:4], inside_ref, whole_ref)
+    values = [ref[...] for ref in rest[:4]]
+    rates = values[0][values[0].shape[0] // 2 :]
+    near_sums(False, tokens, position_ref, rates, values, inside_ref, whole_ref)
     pair_ref[0] = own_ref[...]
     pair_ref[1] = arrived_ref[...]
 
@@ -169,15 +170,27 @@
     stack_blocks(refs[:5], refs[5])
 
 
-def weight_part(position_ref, turned_ref, own_ref, other_ref, out_ref, token_ref):
+def weight_part(position_ref, turned_ref, own_ref, other_ref, out_ref, token_ref, results, semaphores):
     place = position_ref[0]
+    rank = position_ref[1]
+    copies = []
     for ref, flip in ((own_ref, 0), (other_ref, 1)):
         for index, mask in enumerate(CHIP_MASKS):
-            target = place ^ (mask | flip)
-            out_ref[target & 7, lax.shift_right_logical(target, 3)] = jnp.dot(
+            slot = mask | flip
+            target = place ^ slot
+            results[slot] = jnp.dot(
                 turned_ref[...], ref[index], preferred_element_type=F32
             ).astype(BF16)
+            copy = pltpu.make_async_copy(
+                results.at[slot],
+                out_ref.at[target & 7, lax.shift_right_logical(target ^ rank, 3)],
+                semaphores.at[slot],
+            )
+            copy.start()
+            copies.append(copy)
     token_ref[...] = jnp.zeros(token_ref.shape, F32)
+    for copy in copies:
+        copy.wait()
 
 
 def project_rows(position_ref, query_ref, mixed_ref, gated_ref, out_weight_ref, own_ref, other_ref, query_grad_ref, drive_ref, sent_ref, mine_ref):
@@ -287,18 +300,14 @@
 
 
 def backward_near(tokens, position_ref, rate_ref, *rest):
-    near_sums(True, tokens, position_ref, rate_ref, rest[:4], rest[4], rest[5])
+    values = [ref[...] for ref in rest[:4]]
+    near_sums(True, tokens, position_ref, rate_ref[...], values, rest[4], rest[5])
 
 
 def merge_near(rest_ref, first_ref, third_ref, kept_ref, sent_ref):
     for index, ref in enumerate((kept_ref, sent_ref)):
         total = widened(rest_ref, index) + widened(first_ref, index) + widened(third_ref, index)
         ref[...] = total.astype(ref.dtype)
-
-
-def join_weight(position_ref, kept_ref, arrived_ref, out_ref):
-    side = lax.shift_right_logical(position_ref[1], 3)
-    out_ref[...] = kept_ref[side].astype(F32) + widened(arrived_ref)
 
 
 def merge_last(kept_ref, arrived_ref, out_ref):
@@ -380,8 +389,8 @@
         functools.partial(forward_local, tokens * ctx_count),
         grid=(tiles,),
         in_specs=[rows, rows, few, few, one],
-        out_specs=[few, rows, few, few, few],
-        out_shape=[state_shape, square, state_shape, state_shape, state_shape],
+        out_specs=[tile_of(2 * modes), rows, few, few, few],
+        out_shape=[shape_of(2 * modes, width), square, state_shape, state_shape, state_shape],
         scratch_shapes=[block_scratch] * 3,
         name="forward_local",
     )(key_rows, value_rows, decays, residues, skip_row)
@@ -390,7 +399,6 @@
         functools.partial(forward_near, tokens),
         [state_shape, state_shape, pair_block],
         positions,
-        rates,
         *near,
         cotangent,
         arrived,
@@ -419,15 +427,18 @@
     own = local_call(stack_arrived, [eight], pair, first, third, even, odd)[0]
 
     sibling = traded(own, "chan", 1)
-    weight_share, token = local_call(
+    weight_share, token = pl.pallas_call(
         weight_part,
-        [kind_of(8, 2, width, columns), shape_of(HALF, LANES)],
-        positions,
-        gated_turned,
-        own,
-        sibling,
-        scalars=1,
-    )
+        in_specs=[SMEM] + [VMEM] * 3,
+        out_specs=[pl.BlockSpec(memory_space=pltpu.HBM), VMEM],
+        out_shape=[pltpu.HBM((8, 2, width, columns), BF16), shape_of(HALF, LANES)],
+        scratch_shapes=[
+            pltpu.VMEM((ctx_count, width, columns), BF16),
+            pltpu.SemaphoreType.DMA((ctx_count,)),
+        ],
+        compiler_params=granted(11),
+        name="weight_part",
+    )(positions, gated_turned, own, sibling)
     weight_grad = lax.psum_scatter(
         weight_share,
         "ctx",
@@ -511,20 +522,8 @@
         scratch_shapes=[block_scratch] * 2,
         name="backward_mix",
     )(positions, back_local, key_rows, value_rows, rates, weights, inside, whole, *across)
-    side = lax.axis_index("ctx") >> 3
-    whole_of = lambda *shape: pl.BlockSpec(shape, lambda step: (0,) * len(shape))
-    weight_grad = pl.pallas_call(
-        join_weight,
-        grid=(1,),
-        in_specs=[SMEM, whole_of(2, width, columns), whole_of(width, columns)],
-        out_specs=whole_of(width, columns),
-        out_shape=shape_of(width, columns),
-        name="join_weight",
-    )(
-        positions,
-        weight_grad,
-        traded(lax.dynamic_index_in_dim(weight_grad, 1 - side, 0, keepdims=False), "ctx", 8),
-    )
+    arrived = traded(weight_grad[1], "ctx", 8)
+    weight_grad = weight_grad[0].astype(F32) + arrived.astype(F32)
     return (
         layer_out,
         query_grad,

time: 133 us -> 130 us (0.977)
  local copies, waits for them, and re-layouts: 17.9 us -> 11 us
  waiting for transfers between devices: 38.5 us -> 43.9 us
  Pallas kernels: 21.5 us -> 19 us
    unnamed x54 -> x44, local copies, waits for them, and re-layouts: 16.9 us -> 9.98 us
    reduce_scatter x1, waiting for transfers between devices: 4.29 us -> 9.83 us  [on_device(): lax.psum_scatter(weight_share, 'ctx', scatter_dimension=0, axis_index_gro...]
    pallas_call x11 -> x10, Pallas kernels: 11.6 us -> 8.22 us  [ordered_call(): pl.pallas_call(skipping, in_specs=[ANY] * count + in_specs, **options)]
  transfers between devices with their start and end apart: 26 -> 26, of which waited for: 16 -> 16; matrix products, arithmetic and copies ran while one was open for 1% -> 1% of each run, Pallas kernels for 13% -> 12%
where the time goes in v2:
time: 130 us; the launch traced here: 129 us
  waiting for transfers between devices  43.9 us (34%)
  starting transfers between devices  39.8 us (31%)
  Pallas kernels  19 us (15%)
  between operations  14.3 us (11%)
  local copies, waits for them, and re-layouts  11 us (8%)
    ppermute x25, starting transfers between devices, traded(): return lax.ppermute(value, axis, pairs)  39.8 us
    ppermute x25, waiting for transfers between devices, traded(): return lax.ppermute(value, axis, pairs)  34 us
    unnamed x44, local copies, waits for them, and re-layouts  9.98 us
    reduce_scatter x1, waiting for transfers between devices, on_device(): lax.psum_scatter(weight_share, 'ctx', scatter_dimension=0, axis_index_gro...  9.83 us
    pallas_call x10, Pallas kernels, ordered_call(): pl.pallas_call(skipping, in_specs=[ANY] * count + in_specs, **options)  8.22 us
    pallas_call x1, Pallas kernels, on_device(): pl.pallas_call(backward_local, grid=(tiles,), in_specs=[rows, rows, rows,...  3.1 us
    pallas_call x1, Pallas kernels, on_device(): pl.pallas_call(weight_part, in_specs=[SMEM] + [VMEM] * 3, out_specs=[pl.B...  2.93 us
  transfers between devices with their start and end apart: 26, of which 16 were waited for; matrix products, arithmetic and copies ran while one was open for 1% of the time, Pallas kernels for 12%

profile of v2, /device:TPU:14, one launch (start us, length us, event | category | flops | bytes accessed | tf_op | source)
XLA Modules:
  0.0 128.9 jit_solution(5467703946942882828)
XLA Ops:
  7.2 2.4 %collective-permute-start.3 = (bf16[256,512]{1,0:T(8,128)(2,1)}, bf16[256,512]{1,0:T(8,128)(2,1)S(1)}, u32[]{:S(2)}, u32[]{:S(2)}) collective-permute-start(bf16[256,512]{1,0:T(8,128)(2,1)} %refs_5_.2), channel_id=1, source_target_pairs={{0,2},{1,3},{2,0},{3,1},{4,6},{5,7},{6,4},{7,5},{8,10},{9,11},{10,... | collective-permute-start | bytes 786440 | tf_op jit(solution)/shard_map/ppermute | solution.py:20
  9.6 2.5 %forward_local.1 = (f32[32,256]{1,0:T(8,128)}, f32[256,256]{1,0:T(8,128)}, f32[16,256]{1,0:T(8,128)}, f32[16,256]{1,0:T(8,128)}, f32[16,256]{1,0:T(8,128)}) custom-call(bf16[256,256]{1,0:T(8,128)(2,1)} %key_ref.5, bf16[256,256]{1,0:T(8,128)(2,1)} %value_ref.5, f32[16,256]{1,0:T(8,128)} %decay_ref.1, f32[16,256]{1,0:T(8,128)} %residue_ref.1, f32[1,256]{1,0:T(1,128)} %bitcast.11), custom_call_target="tpu_custom_call" | custom-call | tf_op jit(solution)/shard_map/forward_local/pallas_call | solution.py:388
  12.1 4.7 %collective-permute-start.2 = (f32[32,256]{1,0:T(8,128)}, f32[32,256]{1,0:T(8,128)S(1)}, u32[]{:S(2)}, u32[]{:S(2)}) collective-permute-start(f32[32,256]{1,0:T(8,128)} %get-tuple-element.43.refs_1_), channel_id=1, source_target_pairs={{0,48},{16,32},{32,16},{48,0},{64,112},{80,96},{96,80},{112,64},{1... | collective-permute-start | bytes 98312 | tf_op jit(solution)/shard_map/ppermute | solution.py:20
  19.3 2.6 %collective-permute-done.1.refs_3_ = f32[32,256]{1,0:T(8,128)S(1)} collective-permute-done((f32[32,256]{1,0:T(8,128)}, f32[32,256]{1,0:T(8,128)S(1)}, u32[]{:S(2)}, u32[]{:S(2)}) %collective-permute-start.1) | collective-permute-done | bytes 32800 | tf_op jit(solution)/shard_map/ppermute | solution.py:20
  25.6 5.4 %collective-permute-start.6 = (f32[16,256]{1,0:T(8,128)S(1)}, f32[16,256]{1,0:T(8,128)S(1)}, u32[]{:S(2)}, u32[]{:S(2)}) collective-permute-start(f32[16,256]{1,0:T(8,128)S(1)} %get-tuple-element.44), channel_id=1, source_target_pairs={{0,192},{16,208},{32,224},{48,240},{64,128},{80,144},{96,160},{112... | collective-permute-start | bytes 49160 | tf_op jit(solution)/shard_map/ppermute | solution.py:20
  34.8 4.6 %collective-permute-done.4.refs_0_.refs_7_ = f32[16,256]{1,0:T(8,128)S(1)} collective-permute-done((f32[16,256]{1,0:T(8,128)S(1)}, f32[16,256]{1,0:T(8,128)S(1)}, u32[]{:S(2)}, u32[]{:S(2)}) %collective-permute-start.4) | collective-permute-done | bytes 16416 | tf_op jit(solution)/shard_map/ppermute | solution.py:20
  40.6 2.8 %collective-permute-start.9 = (bf16[256,512]{1,0:T(8,128)(2,1)S(1)}, bf16[256,512]{1,0:T(8,128)(2,1)S(1)}, u32[]{:S(2)}, u32[]{:S(2)}) collective-permute-start(bf16[256,512]{1,0:T(8,128)(2,1)S(1)} %get-tuple-element.46.refs_0_), channel_id=1, source_target_pairs={{0,12},{1,13},{2,14},{3,15},{4,8},{5,9},{6,10},{7,11},{8,4},{9,5},... | collective-permute-start | bytes 786440 | tf_op jit(solution)/shard_map/ppermute | solution.py:20
  43.5 2.4 %collective-permute-done.10.refs_4_ = bf16[256,512]{1,0:T(8,128)(2,1)S(1)} collective-permute-done((bf16[256,512]{1,0:T(8,128)(2,1)S(1)}, bf16[256,512]{1,0:T(8,128)(2,1)S(1)}, u32[]{:S(2)}, u32[]{:S(2)}) %collective-permute-start.10) | collective-permute-done | bytes 262176 | tf_op jit(solution)/shard_map/ppermute | solution.py:20
  45.9 2.4 %collective-permute-done.9.refs_3_ = bf16[256,512]{1,0:T(8,128)(2,1)S(1)} collective-permute-done((bf16[256,512]{1,0:T(8,128)(2,1)S(1)}, bf16[256,512]{1,0:T(8,128)(2,1)S(1)}, u32[]{:S(2)}, u32[]{:S(2)}) %collective-permute-start.9) | collective-permute-done | bytes 262176 | tf_op jit(solution)/shard_map/ppermute | solution.py:20
  50.1 2.8 %collective-permute-done.11.other_ref.refs_7_ = bf16[8,256,512]{2,1,0:T(8,128)(2,1)S(1)} collective-permute-done((bf16[8,256,512]{2,1,0:T(8,128)(2,1)S(1)}, bf16[8,256,512]{2,1,0:T(8,128)(2,1)S(1)}, u32[]{:S(2)}, u32[]{:S(2)}) %collective-permute-start.11) | collective-permute-done | bytes 2097184 | tf_op jit(solution)/shard_map/ppermute | solution.py:20
  52.9 2.9 %weight_part.1 = (bf16[8,2,256,512]{3,2,1,0:T(8,128)(2,1)}, f32[8,128]{1,0:T(8,128)S(1)}) custom-call(s32[2]{0:T(128)S(1)} %pad_add_fusion.refs_0_.refs_1_.position_ref, bf16[256,256]{1,0:T(8,128)(2,1)S(1)} %get-tuple-element.50.turned_ref, bf16[8,256,512]{2,1,0:T(8,128)(2,1)S(1)} %stack_arrived.1.own_ref.refs_6_, ...), custom_call_target="tpu_custom_call" | custom-call | tf_op jit(solution)/shard_map/weight_part/pallas_call | solution.py:430
  57.5 2.2 %copy-done.2 = bf16[256,8192]{1,0:T(8,128)(2,1)S(1)} copy-done((bf16[256,8192]{1,0:T(8,128)(2,1)S(1)}, bf16[256,8192]{1,0:T(8,128)(2,1)}, u32[]{:S(2)}) %copy-start.2) | copy-done | bytes 4194328
  59.6 4.0 %project_rows.1 = (bf16[256,256]{1,0:T(8,128)(2,1)}, f32[256,256]{1,0:T(8,128)S(1)}, bf16[8,256,512]{2,1,0:T(8,128)(2,1)}, bf16[8,256,512]{2,1,0:T(8,128)(2,1)S(1)}) custom-call(f32[8,128]{1,0:T(8,128)S(1)} %get-tuple-element.52.refs_0_, s32[2]{0:T(128)S(1)} %pad_add_fusion.refs_0_.refs_1_.position_ref, bf16[256,256]{1,0:T(8,128)(2,1)S(1)} %copy-done.5, ...), custom_call_target="tpu_custom_call" | custom-call | tf_op jit(solution)/shard_map/project_rows/pallas_call | solution.py:336
  65.8 3.1 %backward_local.1 = (f32[256,256]{1,0:T(8,128)}, f32[40,256]{1,0:T(8,128)}) custom-call(f32[256,256]{1,0:T(8,128)} %copy-done.8, bf16[256,256]{1,0:T(8,128)(2,1)} %key_ref.5, bf16[256,256]{1,0:T(8,128)(2,1)} %value_ref.5, f32[16,256]{1,0:T(8,128)} %get-tuple-element.42.refs_4_.rate_ref.refs_1_, f32[16,256]{1,0:T(8,128)} %get-tuple-element.48.refs_5_.weight_ref, ...), custom_call_target="tpu_custom_call" | custom-call | tf_op jit(solution)/shard_map/backward_local/pallas_call | solution.py:463
  73.1 2.9 %collective-permute-start.20 = (bf16[256,512]{1,0:T(8,128)(2,1)S(1)}, bf16[256,512]{1,0:T(8,128)(2,1)S(1)}, u32[]{:S(2)}, u32[]{:S(2)}) collective-permute-start(bf16[256,512]{1,0:T(8,128)(2,1)S(1)} %get-tuple-element.64), channel_id=1, source_target_pairs={{0,12},{1,13},{2,14},{3,15},{4,8},{5,9},{6,10},{7,11},{8,4},{9,5},... | collective-permute-start | bytes 786440 | tf_op jit(solution)/shard_map/ppermute | solution.py:20
  80.4 2.8 %collective-permute-done.14.refs_5_ = f32[40,256]{1,0:T(8,128)S(1)} collective-permute-done((f32[40,256]{1,0:T(8,128)S(1)}, f32[40,256]{1,0:T(8,128)S(1)}, u32[]{:S(2)}, u32[]{:S(2)}) %collective-permute-start.14) | collective-permute-done | bytes 40992 | tf_op jit(solution)/shard_map/ppermute | solution.py:20
  83.1 2.1 %collective-permute-done.13.refs_4_ = f32[40,256]{1,0:T(8,128)S(1)} collective-permute-done((f32[40,256]{1,0:T(8,128)S(1)}, f32[40,256]{1,0:T(8,128)S(1)}, u32[]{:S(2)}, u32[]{:S(2)}) %collective-permute-start.13) | collective-permute-done | bytes 40992 | tf_op jit(solution)/shard_map/ppermute | solution.py:20
  88.1 2.6 %collective-permute-start.17 = (f32[40,256]{1,0:T(8,128)S(1)}, f32[40,256]{1,0:T(8,128)S(1)}, u32[]{:S(2)}, u32[]{:S(2)}) collective-permute-start(f32[40,256]{1,0:T(8,128)S(1)} %get-tuple-element.59.refs_0_.whole_ref), channel_id=1, source_target_pairs={{0,192},{16,208},{32,224},{48,240},{64,128},{80,144},{96,160},{112... | collective-permute-start | bytes 122888 | tf_op jit(solution)/shard_map/ppermute | solution.py:20
  91.4 4.1 %collective-permute-start.15 = (f32[40,256]{1,0:T(8,128)S(1)}, f32[40,256]{1,0:T(8,128)S(1)}, u32[]{:S(2)}, u32[]{:S(2)}) collective-permute-start(f32[40,256]{1,0:T(8,128)S(1)} %get-tuple-element.59.refs_0_.whole_ref), channel_id=1, source_target_pairs={{0,64},{16,80},{32,96},{48,112},{64,0},{80,16},{96,32},{112,48},{1... | collective-permute-start | bytes 122888 | tf_op jit(solution)/shard_map/ppermute | solution.py:20
  95.5 3.1 %collective-permute-done.17.refs_2_.third_ref = f32[40,256]{1,0:T(8,128)S(1)} collective-permute-done((f32[40,256]{1,0:T(8,128)S(1)}, f32[40,256]{1,0:T(8,128)S(1)}, u32[]{:S(2)}, u32[]{:S(2)}) %collective-permute-start.17) | collective-permute-done | bytes 40992 | tf_op jit(solution)/shard_map/ppermute | solution.py:20
  98.6 2.0 %collective-permute-done.15.refs_0_.first_ref = f32[40,256]{1,0:T(8,128)S(1)} collective-permute-done((f32[40,256]{1,0:T(8,128)S(1)}, f32[40,256]{1,0:T(8,128)S(1)}, u32[]{:S(2)}, u32[]{:S(2)}) %collective-permute-start.15) | collective-permute-done | bytes 40992 | tf_op jit(solution)/shard_map/ppermute | solution.py:20
  102.5 9.8 %reduce-scatter.2.cloned.1.call-done = bf16[1,2,256,512]{3,2,1,0:T(8,128)(2,1)} async-done(((bf16[8,2,256,512]{3,2,1,0:T(8,128)(2,1)}), bf16[1,2,256,512]{3,2,1,0:T(8,128)(2,1)}) %reduce-scatter.2.cloned.1.call-update) | async-done | bytes 524304 | tf_op jit(solution)/shard_map/reduce_scatter | solution.py:442
  114.0 2.2 %backward_mix.1 = (bf16[256,256]{1,0:T(8,128)(2,1)}, bf16[256,256]{1,0:T(8,128)(2,1)}, f32[16,256]{1,0:T(8,128)}, f32[1,256]{1,0:T(1,128)}) custom-call(s32[2]{0:T(128)} %copy-done.18, f32[256,256]{1,0:T(8,128)} %get-tuple-element.70.local_ref, bf16[256,256]{1,0:T(8,128)(2,1)} %key_ref.5, bf16[256,256]{1,0:T(8,128)(2,1)} %value_ref.5, ...), custom_call_target="tpu_custom_call" | custom-call | tf_op jit(solution)/shard_map/backward_mix/pallas_call | solution.py:511
  117.0 4.2 %collective-permute-done.24 = bf16[256,512]{1,0:T(8,128)(2,1)S(1)} collective-permute-done((bf16[256,512]{1,0:T(8,128)(2,1)S(1)}, bf16[256,512]{1,0:T(8,128)(2,1)S(1)}, u32[]{:S(2)}, u32[]{:S(2)}) %collective-permute-start.24) | collective-permute-done | bytes 262176 | tf_op jit(solution)/shard_map/ppermute | solution.py:20
  (90 shorter events, 33.7 us)
Async XLA Ops:
  7.2 105.1 %reduce-scatter.2.cloned.1.call-start = ((), (), s32[]{:S(2)}) async-start(), calls=%async_computation.1 | async-start | bytes 4718592 | tf_op jit(solution)/shard_map/reduce_scatter | solution.py:442
  7.2 14.7 %collective-permute-start.3 = (bf16[256,512]{1,0:T(8,128)(2,1)}, bf16[256,512]{1,0:T(8,128)(2,1)S(1)}, u32[]{:S(2)}, u32[]{:S(2)}) collective-permute-start(bf16[256,512]{1,0:T(8,128)(2,1)} %refs_5_.2), channel_id=1, source_target_pairs={{0,2},{1,3},{2,0},{3,1},{4,6},{5,7},{6,4},{7,5},{8,10},{9,11},{10,... | collective-permute-start | bytes 786440 | tf_op jit(solution)/shard_map/ppermute | solution.py:20
  12.1 7.1 %collective-permute-start.2 = (f32[32,256]{1,0:T(8,128)}, f32[32,256]{1,0:T(8,128)S(1)}, u32[]{:S(2)}, u32[]{:S(2)}) collective-permute-start(f32[32,256]{1,0:T(8,128)} %get-tuple-element.43.refs_1_), channel_id=1, source_target_pairs={{0,48},{16,32},{32,16},{48,0},{64,112},{80,96},{96,80},{112,64},{1... | collective-permute-start | bytes 98312 | tf_op jit(solution)/shard_map/ppermute | solution.py:20
  16.8 5.0 %collective-permute-start.1 = (f32[32,256]{1,0:T(8,128)}, f32[32,256]{1,0:T(8,128)S(1)}, u32[]{:S(2)}, u32[]{:S(2)}) collective-permute-start(f32[32,256]{1,0:T(8,128)} %get-tuple-element.43.refs_1_), channel_id=1, source_target_pairs={{0,32},{16,48},{32,0},{48,16},{64,96},{80,112},{96,64},{112,80},{1... | collective-permute-start | bytes 98312 | tf_op jit(solution)/shard_map/ppermute | solution.py:20
  16.8 5.0 %collective-permute-start = (f32[32,256]{1,0:T(8,128)}, f32[32,256]{1,0:T(8,128)S(1)}, u32[]{:S(2)}, u32[]{:S(2)}) collective-permute-start(f32[32,256]{1,0:T(8,128)} %get-tuple-element.43.refs_1_), channel_id=1, source_target_pairs={{0,16},{16,0},{32,48},{48,32},{64,80},{80,64},{96,112},{112,96},{1... | collective-permute-start | bytes 98312 | tf_op jit(solution)/shard_map/ppermute | solution.py:20
  24.2 15.2 %collective-permute-start.8 = (bf16[2,256,512]{2,1,0:T(8,128)(2,1)S(1)}, bf16[2,256,512]{2,1,0:T(8,128)(2,1)S(1)}, u32[]{:S(2)}, u32[]{:S(2)}) collective-permute-start(bf16[2,256,512]{2,1,0:T(8,128)(2,1)S(1)} %get-tuple-element.45.refs_0_), channel_id=1, source_target_pairs={{0,12},{1,13},{2,14},{3,15},{4,8},{5,9},{6,10},{7,11},{8,4},{9,5},... | collective-permute-start | bytes 1572872 | tf_op jit(solution)/shard_map/ppermute | solution.py:20
  24.7 14.6 %collective-permute-start.7 = (bf16[2,256,512]{2,1,0:T(8,128)(2,1)S(1)}, bf16[2,256,512]{2,1,0:T(8,128)(2,1)S(1)}, u32[]{:S(2)}, u32[]{:S(2)}) collective-permute-start(bf16[2,256,512]{2,1,0:T(8,128)(2,1)S(1)} %get-tuple-element.45.refs_0_), channel_id=1, source_target_pairs={{0,4},{1,5},{2,6},{3,7},{4,0},{5,1},{6,2},{7,3},{8,12},{9,13},{10,... | collective-permute-start | bytes 1572872 | tf_op jit(solution)/shard_map/ppermute | solution.py:20
  25.6 8.5 %collective-permute-start.6 = (f32[16,256]{1,0:T(8,128)S(1)}, f32[16,256]{1,0:T(8,128)S(1)}, u32[]{:S(2)}, u32[]{:S(2)}) collective-permute-start(f32[16,256]{1,0:T(8,128)S(1)} %get-tuple-element.44), channel_id=1, source_target_pairs={{0,192},{16,208},{32,224},{48,240},{64,128},{80,144},{96,160},{112... | collective-permute-start | bytes 49160 | tf_op jit(solution)/shard_map/ppermute | solution.py:20
  31.7 7.6 %collective-permute-start.4 = (f32[16,256]{1,0:T(8,128)S(1)}, f32[16,256]{1,0:T(8,128)S(1)}, u32[]{:S(2)}, u32[]{:S(2)}) collective-permute-start(f32[16,256]{1,0:T(8,128)S(1)} %get-tuple-element.44), channel_id=1, source_target_pairs={{0,64},{16,80},{32,96},{48,112},{64,0},{80,16},{96,32},{112,48},{1... | collective-permute-start | bytes 49160 | tf_op jit(solution)/shard_map/ppermute | solution.py:20
  39.4 6.5 %collective-permute-start.10 = (bf16[256,512]{1,0:T(8,128)(2,1)S(1)}, bf16[256,512]{1,0:T(8,128)(2,1)S(1)}, u32[]{:S(2)}, u32[]{:S(2)}) collective-permute-start(bf16[256,512]{1,0:T(8,128)(2,1)S(1)} %get-tuple-element.51), channel_id=1, source_target_pairs={{0,4},{1,5},{2,6},{3,7},{4,0},{5,1},{6,2},{7,3},{8,12},{9,13},{10,... | collective-permute-start | bytes 786440 | tf_op jit(solution)/shard_map/ppermute | solution.py:20
  40.6 7.7 %collective-permute-start.9 = (bf16[256,512]{1,0:T(8,128)(2,1)S(1)}, bf16[256,512]{1,0:T(8,128)(2,1)S(1)}, u32[]{:S(2)}, u32[]{:S(2)}) collective-permute-start(bf16[256,512]{1,0:T(8,128)(2,1)S(1)} %get-tuple-element.46.refs_0_), channel_id=1, source_target_pairs={{0,12},{1,13},{2,14},{3,15},{4,8},{5,9},{6,10},{7,11},{8,4},{9,5},... | collective-permute-start | bytes 786440 | tf_op jit(solution)/shard_map/ppermute | solution.py:20
  48.4 4.4 %collective-permute-start.11 = (bf16[8,256,512]{2,1,0:T(8,128)(2,1)S(1)}, bf16[8,256,512]{2,1,0:T(8,128)(2,1)S(1)}, u32[]{:S(2)}, u32[]{:S(2)}) collective-permute-start(bf16[8,256,512]{2,1,0:T(8,128)(2,1)S(1)} %stack_arrived.1.own_ref.refs_6_), channel_id=1, source_target_pairs={{0,1},{1,0},{2,3},{3,2},{4,5},{5,4},{6,7},{7,6},{8,9},{9,8},{10,11... | collective-permute-start | bytes 6291464 | tf_op jit(solution)/shard_map/ppermute | solution.py:20
  73.0 12.9 %collective-permute-start.19 = (bf16[256,512]{1,0:T(8,128)(2,1)S(1)}, bf16[256,512]{1,0:T(8,128)(2,1)S(1)}, u32[]{:S(2)}, u32[]{:S(2)}) collective-permute-start(bf16[256,512]{1,0:T(8,128)(2,1)S(1)} %get-tuple-element.63), channel_id=1, source_target_pairs={{0,4},{1,5},{2,6},{3,7},{4,0},{5,1},{6,2},{7,3},{8,12},{9,13},{10,... | collective-permute-start | bytes 786440 | tf_op jit(solution)/shard_map/ppermute | solution.py:20
  73.1 12.8 %collective-permute-start.20 = (bf16[256,512]{1,0:T(8,128)(2,1)S(1)}, bf16[256,512]{1,0:T(8,128)(2,1)S(1)}, u32[]{:S(2)}, u32[]{:S(2)}) collective-permute-start(bf16[256,512]{1,0:T(8,128)(2,1)S(1)} %get-tuple-element.64), channel_id=1, source_target_pairs={{0,12},{1,13},{2,14},{3,15},{4,8},{5,9},{6,10},{7,11},{8,4},{9,5},... | collective-permute-start | bytes 786440 | tf_op jit(solution)/shard_map/ppermute | solution.py:20
  76.0 7.2 %collective-permute-start.14 = (f32[40,256]{1,0:T(8,128)S(1)}, f32[40,256]{1,0:T(8,128)S(1)}, u32[]{:S(2)}, u32[]{:S(2)}) collective-permute-start(f32[40,256]{1,0:T(8,128)S(1)} %copy-done.11), channel_id=1, source_target_pairs={{0,48},{16,32},{32,16},{48,0},{64,112},{80,96},{96,80},{112,64},{1... | collective-permute-start | bytes 122888 | tf_op jit(solution)/shard_map/ppermute | solution.py:20
  77.9 7.4 %collective-permute-start.13 = (f32[40,256]{1,0:T(8,128)S(1)}, f32[40,256]{1,0:T(8,128)S(1)}, u32[]{:S(2)}, u32[]{:S(2)}) collective-permute-start(f32[40,256]{1,0:T(8,128)S(1)} %copy-done.11), channel_id=1, source_target_pairs={{0,32},{16,48},{32,0},{48,16},{64,96},{80,112},{96,64},{112,80},{1... | collective-permute-start | bytes 122888 | tf_op jit(solution)/shard_map/ppermute | solution.py:20
  78.9 6.4 %collective-permute-start.12 = (f32[40,256]{1,0:T(8,128)S(1)}, f32[40,256]{1,0:T(8,128)S(1)}, u32[]{:S(2)}, u32[]{:S(2)}) collective-permute-start(f32[40,256]{1,0:T(8,128)S(1)} %copy-done.11), channel_id=1, source_target_pairs={{0,16},{16,0},{32,48},{48,32},{64,80},{80,64},{96,112},{112,96},{1... | collective-permute-start | bytes 122888 | tf_op jit(solution)/shard_map/ppermute | solution.py:20
  86.1 14.6 %collective-permute-start.21 = (bf16[2,256,512]{2,1,0:T(8,128)(2,1)S(1)}, bf16[2,256,512]{2,1,0:T(8,128)(2,1)S(1)}, u32[]{:S(2)}, u32[]{:S(2)}) collective-permute-start(bf16[2,256,512]{2,1,0:T(8,128)(2,1)S(1)} %get-tuple-element.65), channel_id=1, source_target_pairs={{0,4},{1,5},{2,6},{3,7},{4,0},{5,1},{6,2},{7,3},{8,12},{9,13},{10,... | collective-permute-start | bytes 1572872 | tf_op jit(solution)/shard_map/ppermute | solution.py:20
  87.4 13.5 %collective-permute-start.22 = (bf16[2,256,512]{2,1,0:T(8,128)(2,1)S(1)}, bf16[2,256,512]{2,1,0:T(8,128)(2,1)S(1)}, u32[]{:S(2)}, u32[]{:S(2)}) collective-permute-start(bf16[2,256,512]{2,1,0:T(8,128)(2,1)S(1)} %get-tuple-element.66), channel_id=1, source_target_pairs={{0,12},{1,13},{2,14},{3,15},{4,8},{5,9},{6,10},{7,11},{8,4},{9,5},... | collective-permute-start | bytes 1572872 | tf_op jit(solution)/shard_map/ppermute | solution.py:20
  88.1 10.5 %collective-permute-start.17 = (f32[40,256]{1,0:T(8,128)S(1)}, f32[40,256]{1,0:T(8,128)S(1)}, u32[]{:S(2)}, u32[]{:S(2)}) collective-permute-start(f32[40,256]{1,0:T(8,128)S(1)} %get-tuple-element.59.refs_0_.whole_ref), channel_id=1, source_target_pairs={{0,192},{16,208},{32,224},{48,240},{64,128},{80,144},{96,160},{112... | collective-permute-start | bytes 122888 | tf_op jit(solution)/shard_map/ppermute | solution.py:20
  90.7 8.0 %collective-permute-start.16 = (f32[40,256]{1,0:T(8,128)S(1)}, f32[40,256]{1,0:T(8,128)S(1)}, u32[]{:S(2)}, u32[]{:S(2)}) collective-permute-start(f32[40,256]{1,0:T(8,128)S(1)} %get-tuple-element.59.refs_0_.whole_ref), channel_id=1, source_target_pairs={{0,128},{16,144},{32,160},{48,176},{64,192},{80,208},{96,224},{112... | collective-permute-start | bytes 122888 | tf_op jit(solution)/shard_map/ppermute | solution.py:20
  91.4 9.3 %collective-permute-start.15 = (f32[40,256]{1,0:T(8,128)S(1)}, f32[40,256]{1,0:T(8,128)S(1)}, u32[]{:S(2)}, u32[]{:S(2)}) collective-permute-start(f32[40,256]{1,0:T(8,128)S(1)} %get-tuple-element.59.refs_0_.whole_ref), channel_id=1, source_target_pairs={{0,64},{16,80},{32,96},{48,112},{64,0},{80,16},{96,32},{112,48},{1... | collective-permute-start | bytes 122888 | tf_op jit(solution)/shard_map/ppermute | solution.py:20
  101.1 15.1 %collective-permute-start.23 = (bf16[256,512]{1,0:T(8,128)(2,1)S(1)}, bf16[256,512]{1,0:T(8,128)(2,1)S(1)}, u32[]{:S(2)}, u32[]{:S(2)}) collective-permute-start(bf16[256,512]{1,0:T(8,128)(2,1)S(1)} %get-tuple-element.68), channel_id=1, source_target_pairs={{0,2},{1,3},{2,0},{3,1},{4,6},{5,7},{6,4},{7,5},{8,10},{9,11},{10,... | collective-permute-start | bytes 786440 | tf_op jit(solution)/shard_map/ppermute | solution.py:20
  113.3 7.9 %collective-permute-start.24 = (bf16[256,512]{1,0:T(8,128)(2,1)S(1)}, bf16[256,512]{1,0:T(8,128)(2,1)S(1)}, u32[]{:S(2)}, u32[]{:S(2)}) collective-permute-start(bf16[256,512]{1,0:T(8,128)(2,1)S(1)} %slice_bitcast_fusion), channel_id=1, source_target_pairs={{0,128},{16,144},{32,160},{48,176},{64,192},{80,208},{96,224},{112... | collective-permute-start | bytes 786440 | tf_op jit(solution)/shard_map/ppermute | solution.py:20
  (24 other events, 223.0 us)
Sparse Core Ops, SparseCore 0:
  56.0 56.2 reduce-scatter.1

commit v3 on v2

--- a/solution.py
+++ b/solution.py
@@ -31,14 +31,29 @@
     return jnp.where(value < 0.5, value * series, 1.0 - jnp.exp(-value))
 
 
-def forward_local(length, key_ref, value_ref, decay_ref, residue_ref, skip_ref, state_ref, mixed_ref, rate_ref, gain_ref, weight_ref, product, carried, scaled):
+def forward_state(length, key_ref, value_ref, decay_ref, residue_ref, state_ref, rate_ref, gain_ref, weight_ref, product):
     product[...] = key_ref[...].astype(F32) * value_ref[...].astype(F32)
     rates = decay_ref[...] * (1.0 / length)
     gains = jnp.sqrt(shortfall(2.0 * rates) * (1.0 / rates.shape[0]))
-    weights = residue_ref[...] * gains
+    pole = jnp.exp(-rates)
+    leap = jnp.exp(-float(SUB) * rates)
+    state = jnp.zeros_like(rates)
+    for block in range(SUB):
+        inner = jnp.broadcast_to(product[pl.ds(block * SUB, 1), :], rates.shape)
+        for step in range(1, SUB):
+            inner = pole * inner + product[pl.ds(block * SUB + step, 1), :]
+        state = leap * state + inner
+    state_ref[pl.ds(0, SUB), :] = state
+    state_ref[pl.ds(SUB, SUB), :] = rates
     rate_ref[...] = rates
     gain_ref[...] = gains
-    weight_ref[...] = weights
+    weight_ref[...] = residue_ref[...] * gains
+
+
+def forward_local(key_ref, value_ref, rate_ref, weight_ref, skip_ref, mixed_ref, token_ref, product, carried, scaled):
+    product[...] = key_ref[...].astype(F32) * value_ref[...].astype(F32)
+    rates = rate_ref[...]
+    weights = weight_ref[...]
     pole = jnp.exp(-rates)
     leap = jnp.exp(-float(SUB) * rates)
     state = jnp.zeros_like(rates)
@@ -48,8 +63,7 @@
         for step in range(1, SUB):
             inner = pole * inner + product[pl.ds(block * SUB + step, 1), :]
         state = leap * state + inner
-    state_ref[pl.ds(0, SUB), :] = state
-    state_ref[pl.ds(SUB, SUB), :] = rates
+    token_ref[...] = jnp.zeros(token_ref.shape, F32)
     taps = []
     power = weights
     for step in range(SUB):
@@ -385,15 +399,24 @@
     tall_shape = shape_of(tall, width)
 
     arrived = traded(cotangent, "chan", 2)
-    state, local, rates, gains, weights = pl.pallas_call(
-        functools.partial(forward_local, tokens * ctx_count),
+    state, rates, gains, weights = pl.pallas_call(
+        functools.partial(forward_state, tokens * ctx_count),
+        grid=(tiles,),
+        in_specs=[rows, rows, few, few],
+        out_specs=[tile_of(2 * modes), few, few, few],
+        out_shape=[shape_of(2 * modes, width), state_shape, state_shape, state_shape],
+        scratch_shapes=[block_scratch],
+        name="forward_state",
+    )(key_rows, value_rows, decays, residues)
+    local, local_token = pl.pallas_call(
+        forward_local,
         grid=(tiles,),
         in_specs=[rows, rows, few, few, one],
-        out_specs=[tile_of(2 * modes), rows, few, few, few],
-        out_shape=[shape_of(2 * modes, width), square, state_shape, state_shape, state_shape],
+        out_specs=[rows, tile_of(HALF)],
+        out_shape=[square, shape_of(HALF, width)],
         scratch_shapes=[block_scratch] * 3,
         name="forward_local",
-    )(key_rows, value_rows, decays, residues, skip_row)
+    )(key_rows, value_rows, rates, weights, skip_row)
     near = [state] + [traded(state, "ctx", mask) for mask in (1, 2, 3)]
     inside, whole, pair = local_call(
         functools.partial(forward_near, tokens),
@@ -402,6 +425,7 @@
         *near,
         cotangent,
         arrived,
+        ordered=[local_token],
         scalars=1,
     )
 

time: 130 us -> 130 us (level)
  waiting for transfers between devices: 43.9 us -> 41.5 us
  Pallas kernels: 19 us -> 20.9 us
    ppermute x25, waiting for transfers between devices: 34 us -> 31.6 us  [traded(): return lax.ppermute(value, axis, pairs)]
    pallas_call x1 -> x2, Pallas kernels: 2.53 us -> 4.37 us  [the longest x1 2.49 us: on_device(): pl.pallas_call(forward_local, grid=(tiles,), in_specs=[rows, rows, few, f...]
    unnamed x44 -> x46, local copies, waits for them, and re-layouts: 9.98 us -> 10.7 us
  transfers between devices with their start and end apart: 26 -> 26, of which waited for: 16 -> 15; matrix products, arithmetic and copies ran while one was open for 1% -> 1% of each run, Pallas kernels for 12% -> 13%
where the time goes in v3:
time: 130 us; the launch traced here: 129 us
  waiting for transfers between devices  41.5 us (32%)
  starting transfers between devices  39.8 us (31%)
  Pallas kernels  20.9 us (16%)
  between operations  14.3 us (11%)
  local copies, waits for them, and re-layouts  11.7 us (9%)
    ppermute x25, starting transfers between devices, traded(): return lax.ppermute(value, axis, pairs)  39.7 us
    ppermute x25, waiting for transfers between devices, traded(): return lax.ppermute(value, axis, pairs)  31.6 us
    unnamed x46, local copies, waits for them, and re-layouts  10.7 us
    reduce_scatter x1, waiting for transfers between devices, on_device(): lax.psum_scatter(weight_share, 'ctx', scatter_dimension=0, axis_index_gro...  9.84 us
    pallas_call x10, Pallas kernels, ordered_call(): pl.pallas_call(skipping, in_specs=[ANY] * count + in_specs, **options)  8.23 us
    pallas_call x1, Pallas kernels, on_device(): pl.pallas_call(backward_local, grid=(tiles,), in_specs=[rows, rows, rows,...  3.1 us
    pallas_call x1, Pallas kernels, on_device(): pl.pallas_call(weight_part, in_specs=[SMEM] + [VMEM] * 3, out_specs=[pl.B...  2.92 us
  transfers between devices with their start and end apart: 26, of which 15 were waited for; matrix products, arithmetic and copies ran while one was open for 1% of the time, Pallas kernels for 13%

profile of v3, /device:TPU:14, one launch (start us, length us, event | category | flops | bytes accessed | tf_op | source)
XLA Modules:
  0.0 129.0 jit_solution(8324469161429649036)
XLA Ops:
  7.2 2.4 %collective-permute-start.3 = (bf16[256,512]{1,0:T(8,128)(2,1)}, bf16[256,512]{1,0:T(8,128)(2,1)S(1)}, u32[]{:S(2)}, u32[]{:S(2)}) collective-permute-start(bf16[256,512]{1,0:T(8,128)(2,1)} %refs_6_.1), channel_id=1, source_target_pairs={{0,2},{1,3},{2,0},{3,1},{4,6},{5,7},{6,4},{7,5},{8,10},{9,11},{10,... | collective-permute-start | bytes 786440 | tf_op jit(solution)/shard_map/ppermute | solution.py:20
  11.5 4.7 %collective-permute-start.2 = (f32[32,256]{1,0:T(8,128)}, f32[32,256]{1,0:T(8,128)S(1)}, u32[]{:S(2)}, u32[]{:S(2)}) collective-permute-start(f32[32,256]{1,0:T(8,128)} %get-tuple-element.46.refs_2_), channel_id=1, source_target_pairs={{0,48},{16,32},{32,16},{48,0},{64,112},{80,96},{96,80},{112,64},{1... | collective-permute-start | bytes 98312 | tf_op jit(solution)/shard_map/ppermute | solution.py:20
  16.9 2.5 %forward_local.1 = (f32[256,256]{1,0:T(8,128)}, f32[8,256]{1,0:T(8,128)}) custom-call(bf16[256,256]{1,0:T(8,128)(2,1)} %key_ref.7, bf16[256,256]{1,0:T(8,128)(2,1)} %value_ref.7, f32[16,256]{1,0:T(8,128)} %get-tuple-element.43.rate_ref.refs_4_.refs_1_, f32[16,256]{1,0:T(8,128)} %get-tuple-element.44.weight_ref.refs_5_, f32[1,256]{1,0:T(1,128)} %bitcast.11), custom_call_target="tpu_custom_call" | custom-call | tf_op jit(solution)/shard_map/forward_local/pallas_call | solution.py:411
  25.7 5.4 %collective-permute-start.6 = (f32[16,256]{1,0:T(8,128)S(1)}, f32[16,256]{1,0:T(8,128)S(1)}, u32[]{:S(2)}, u32[]{:S(2)}) collective-permute-start(f32[16,256]{1,0:T(8,128)S(1)} %get-tuple-element.47), channel_id=1, source_target_pairs={{0,192},{16,208},{32,224},{48,240},{64,128},{80,144},{96,160},{112... | collective-permute-start | bytes 49160 | tf_op jit(solution)/shard_map/ppermute | solution.py:20
  34.8 4.6 %collective-permute-done.4.refs_0_.refs_7_ = f32[16,256]{1,0:T(8,128)S(1)} collective-permute-done((f32[16,256]{1,0:T(8,128)S(1)}, f32[16,256]{1,0:T(8,128)S(1)}, u32[]{:S(2)}, u32[]{:S(2)}) %collective-permute-start.4) | collective-permute-done | bytes 16416 | tf_op jit(solution)/shard_map/ppermute | solution.py:20
  40.7 2.8 %collective-permute-start.9 = (bf16[256,512]{1,0:T(8,128)(2,1)S(1)}, bf16[256,512]{1,0:T(8,128)(2,1)S(1)}, u32[]{:S(2)}, u32[]{:S(2)}) collective-permute-start(bf16[256,512]{1,0:T(8,128)(2,1)S(1)} %get-tuple-element.49.refs_0_), channel_id=1, source_target_pairs={{0,12},{1,13},{2,14},{3,15},{4,8},{5,9},{6,10},{7,11},{8,4},{9,5},... | collective-permute-start | bytes 786440 | tf_op jit(solution)/shard_map/ppermute | solution.py:20
  43.5 2.4 %collective-permute-done.10.refs_4_ = bf16[256,512]{1,0:T(8,128)(2,1)S(1)} collective-permute-done((bf16[256,512]{1,0:T(8,128)(2,1)S(1)}, bf16[256,512]{1,0:T(8,128)(2,1)S(1)}, u32[]{:S(2)}, u32[]{:S(2)}) %collective-permute-start.10) | collective-permute-done | bytes 262176 | tf_op jit(solution)/shard_map/ppermute | solution.py:20
  45.9 2.4 %collective-permute-done.9.refs_3_ = bf16[256,512]{1,0:T(8,128)(2,1)S(1)} collective-permute-done((bf16[256,512]{1,0:T(8,128)(2,1)S(1)}, bf16[256,512]{1,0:T(8,128)(2,1)S(1)}, u32[]{:S(2)}, u32[]{:S(2)}) %collective-permute-start.9) | collective-permute-done | bytes 262176 | tf_op jit(solution)/shard_map/ppermute | solution.py:20
  50.1 2.8 %collective-permute-done.11.other_ref.refs_7_ = bf16[8,256,512]{2,1,0:T(8,128)(2,1)S(1)} collective-permute-done((bf16[8,256,512]{2,1,0:T(8,128)(2,1)S(1)}, bf16[8,256,512]{2,1,0:T(8,128)(2,1)S(1)}, u32[]{:S(2)}, u32[]{:S(2)}) %collective-permute-start.11) | collective-permute-done | bytes 2097184 | tf_op jit(solution)/shard_map/ppermute | solution.py:20
  52.9 2.9 %weight_part.1 = (bf16[8,2,256,512]{3,2,1,0:T(8,128)(2,1)}, f32[8,128]{1,0:T(8,128)S(1)}) custom-call(s32[2]{0:T(128)S(1)} %pad_add_fusion.refs_1_.position_ref.refs_0_, bf16[256,256]{1,0:T(8,128)(2,1)S(1)} %get-tuple-element.52.turned_ref, bf16[8,256,512]{2,1,0:T(8,128)(2,1)S(1)} %stack_arrived.1.own_ref.refs_6_, ...), custom_call_target="tpu_custom_call" | custom-call | tf_op jit(solution)/shard_map/weight_part/pallas_call | solution.py:454
  57.5 2.2 %copy-done.2 = bf16[256,8192]{1,0:T(8,128)(2,1)S(1)} copy-done((bf16[256,8192]{1,0:T(8,128)(2,1)S(1)}, bf16[256,8192]{1,0:T(8,128)(2,1)}, u32[]{:S(2)}) %copy-start.2) | copy-done | bytes 4194328
  59.7 4.1 %project_rows.1 = (bf16[256,256]{1,0:T(8,128)(2,1)}, f32[256,256]{1,0:T(8,128)S(1)}, bf16[8,256,512]{2,1,0:T(8,128)(2,1)}, bf16[8,256,512]{2,1,0:T(8,128)(2,1)S(1)}) custom-call(f32[8,128]{1,0:T(8,128)S(1)} %get-tuple-element.54.refs_0_, s32[2]{0:T(128)S(1)} %pad_add_fusion.refs_1_.position_ref.refs_0_, bf16[256,256]{1,0:T(8,128)(2,1)S(1)} %copy-done.5, ...), custom_call_target="tpu_custom_call" | custom-call | tf_op jit(solution)/shard_map/project_rows/pallas_call | solution.py:350
  65.9 3.1 %backward_local.1 = (f32[256,256]{1,0:T(8,128)}, f32[40,256]{1,0:T(8,128)}) custom-call(f32[256,256]{1,0:T(8,128)} %copy-done.11, bf16[256,256]{1,0:T(8,128)(2,1)} %key_ref.7, bf16[256,256]{1,0:T(8,128)(2,1)} %value_ref.7, f32[16,256]{1,0:T(8,128)} %get-tuple-element.43.rate_ref.refs_4_.refs_1_, f32[16,256]{1,0:T(8,128)} %get-tuple-element.44.weight_ref.refs_5_, ...), custom_call_target="tpu_custom_call" | custom-call | tf_op jit(solution)/shard_map/backward_local/pallas_call | solution.py:487
  73.1 2.9 %collective-permute-start.20 = (bf16[256,512]{1,0:T(8,128)(2,1)S(1)}, bf16[256,512]{1,0:T(8,128)(2,1)S(1)}, u32[]{:S(2)}, u32[]{:S(2)}) collective-permute-start(bf16[256,512]{1,0:T(8,128)(2,1)S(1)} %get-tuple-element.66), channel_id=1, source_target_pairs={{0,12},{1,13},{2,14},{3,15},{4,8},{5,9},{6,10},{7,11},{8,4},{9,5},... | collective-permute-start | bytes 786440 | tf_op jit(solution)/shard_map/ppermute | solution.py:20
  76.0 1.9 %collective-permute-start.14 = (f32[40,256]{1,0:T(8,128)S(1)}, f32[40,256]{1,0:T(8,128)S(1)}, u32[]{:S(2)}, u32[]{:S(2)}) collective-permute-start(f32[40,256]{1,0:T(8,128)S(1)} %copy-done.12), channel_id=1, source_target_pairs={{0,48},{16,32},{32,16},{48,0},{64,112},{80,96},{96,80},{112,64},{1... | collective-permute-start | bytes 122888 | tf_op jit(solution)/shard_map/ppermute | solution.py:20
  80.4 2.8 %collective-permute-done.14.refs_5_ = f32[40,256]{1,0:T(8,128)S(1)} collective-permute-done((f32[40,256]{1,0:T(8,128)S(1)}, f32[40,256]{1,0:T(8,128)S(1)}, u32[]{:S(2)}, u32[]{:S(2)}) %collective-permute-start.14) | collective-permute-done | bytes 40992 | tf_op jit(solution)/shard_map/ppermute | solution.py:20
  83.2 2.1 %collective-permute-done.13.refs_4_ = f32[40,256]{1,0:T(8,128)S(1)} collective-permute-done((f32[40,256]{1,0:T(8,128)S(1)}, f32[40,256]{1,0:T(8,128)S(1)}, u32[]{:S(2)}, u32[]{:S(2)}) %collective-permute-start.13) | collective-permute-done | bytes 40992 | tf_op jit(solution)/shard_map/ppermute | solution.py:20
  88.1 2.6 %collective-permute-start.17 = (f32[40,256]{1,0:T(8,128)S(1)}, f32[40,256]{1,0:T(8,128)S(1)}, u32[]{:S(2)}, u32[]{:S(2)}) collective-permute-start(f32[40,256]{1,0:T(8,128)S(1)} %get-tuple-element.61.refs_0_.whole_ref), channel_id=1, source_target_pairs={{0,192},{16,208},{32,224},{48,240},{64,128},{80,144},{96,160},{112... | collective-permute-start | bytes 122888 | tf_op jit(solution)/shard_map/ppermute | solution.py:20
  91.4 4.1 %collective-permute-start.15 = (f32[40,256]{1,0:T(8,128)S(1)}, f32[40,256]{1,0:T(8,128)S(1)}, u32[]{:S(2)}, u32[]{:S(2)}) collective-permute-start(f32[40,256]{1,0:T(8,128)S(1)} %get-tuple-element.61.refs_0_.whole_ref), channel_id=1, source_target_pairs={{0,64},{16,80},{32,96},{48,112},{64,0},{80,16},{96,32},{112,48},{1... | collective-permute-start | bytes 122888 | tf_op jit(solution)/shard_map/ppermute | solution.py:20
  95.5 3.2 %collective-permute-done.17.refs_2_.third_ref = f32[40,256]{1,0:T(8,128)S(1)} collective-permute-done((f32[40,256]{1,0:T(8,128)S(1)}, f32[40,256]{1,0:T(8,128)S(1)}, u32[]{:S(2)}, u32[]{:S(2)}) %collective-permute-start.17) | collective-permute-done | bytes 40992 | tf_op jit(solution)/shard_map/ppermute | solution.py:20
  98.7 2.0 %collective-permute-done.15.refs_0_.first_ref = f32[40,256]{1,0:T(8,128)S(1)} collective-permute-done((f32[40,256]{1,0:T(8,128)S(1)}, f32[40,256]{1,0:T(8,128)S(1)}, u32[]{:S(2)}, u32[]{:S(2)}) %collective-permute-start.15) | collective-permute-done | bytes 40992 | tf_op jit(solution)/shard_map/ppermute | solution.py:20
  102.5 9.8 %reduce-scatter.2.cloned.1.call-done = bf16[1,2,256,512]{3,2,1,0:T(8,128)(2,1)} async-done(((bf16[8,2,256,512]{3,2,1,0:T(8,128)(2,1)}), bf16[1,2,256,512]{3,2,1,0:T(8,128)(2,1)}) %reduce-scatter.2.cloned.1.call-update) | async-done | bytes 524304 | tf_op jit(solution)/shard_map/reduce_scatter | solution.py:466
  114.0 2.2 %backward_mix.1 = (bf16[256,256]{1,0:T(8,128)(2,1)}, bf16[256,256]{1,0:T(8,128)(2,1)}, f32[16,256]{1,0:T(8,128)}, f32[1,256]{1,0:T(1,128)}) custom-call(s32[2]{0:T(128)} %copy-done.18, f32[256,256]{1,0:T(8,128)} %get-tuple-element.72.local_ref, bf16[256,256]{1,0:T(8,128)(2,1)} %key_ref.7, bf16[256,256]{1,0:T(8,128)(2,1)} %value_ref.7, ...), custom_call_target="tpu_custom_call" | custom-call | tf_op jit(solution)/shard_map/backward_mix/pallas_call | solution.py:535
  117.1 4.2 %collective-permute-done.24 = bf16[256,512]{1,0:T(8,128)(2,1)S(1)} collective-permute-done((bf16[256,512]{1,0:T(8,128)(2,1)S(1)}, bf16[256,512]{1,0:T(8,128)(2,1)S(1)}, u32[]{:S(2)}, u32[]{:S(2)}) %collective-permute-start.24) | collective-permute-done | bytes 262176 | tf_op jit(solution)/shard_map/ppermute | solution.py:20
  (93 shorter events, 34.5 us)
Async XLA Ops:
  7.2 105.2 %reduce-scatter.2.cloned.1.call-start = ((), (), s32[]{:S(2)}) async-start(), calls=%async_computation.1 | async-start | bytes 4718592 | tf_op jit(solution)/shard_map/reduce_scatter | solution.py:466
  7.2 14.0 %collective-permute-start.3 = (bf16[256,512]{1,0:T(8,128)(2,1)}, bf16[256,512]{1,0:T(8,128)(2,1)S(1)}, u32[]{:S(2)}, u32[]{:S(2)}) collective-permute-start(bf16[256,512]{1,0:T(8,128)(2,1)} %refs_6_.1), channel_id=1, source_target_pairs={{0,2},{1,3},{2,0},{3,1},{4,6},{5,7},{6,4},{7,5},{8,10},{9,11},{10,... | collective-permute-start | bytes 786440 | tf_op jit(solution)/shard_map/ppermute | solution.py:20
  11.5 7.9 %collective-permute-start.2 = (f32[32,256]{1,0:T(8,128)}, f32[32,256]{1,0:T(8,128)S(1)}, u32[]{:S(2)}, u32[]{:S(2)}) collective-permute-start(f32[32,256]{1,0:T(8,128)} %get-tuple-element.46.refs_2_), channel_id=1, source_target_pairs={{0,48},{16,32},{32,16},{48,0},{64,112},{80,96},{96,80},{112,64},{1... | collective-permute-start | bytes 98312 | tf_op jit(solution)/shard_map/ppermute | solution.py:20
  16.2 5.0 %collective-permute-start.1 = (f32[32,256]{1,0:T(8,128)}, f32[32,256]{1,0:T(8,128)S(1)}, u32[]{:S(2)}, u32[]{:S(2)}) collective-permute-start(f32[32,256]{1,0:T(8,128)} %get-tuple-element.46.refs_2_), channel_id=1, source_target_pairs={{0,32},{16,48},{32,0},{48,16},{64,96},{80,112},{96,64},{112,80},{1... | collective-permute-start | bytes 98312 | tf_op jit(solution)/shard_map/ppermute | solution.py:20
  16.2 5.0 %collective-permute-start = (f32[32,256]{1,0:T(8,128)}, f32[32,256]{1,0:T(8,128)S(1)}, u32[]{:S(2)}, u32[]{:S(2)}) collective-permute-start(f32[32,256]{1,0:T(8,128)} %get-tuple-element.46.refs_2_), channel_id=1, source_target_pairs={{0,16},{16,0},{32,48},{48,32},{64,80},{80,64},{96,112},{112,96},{1... | collective-permute-start | bytes 98312 | tf_op jit(solution)/shard_map/ppermute | solution.py:20
  24.2 15.2 %collective-permute-start.8 = (bf16[2,256,512]{2,1,0:T(8,128)(2,1)S(1)}, bf16[2,256,512]{2,1,0:T(8,128)(2,1)S(1)}, u32[]{:S(2)}, u32[]{:S(2)}) collective-permute-start(bf16[2,256,512]{2,1,0:T(8,128)(2,1)S(1)} %get-tuple-element.48.refs_0_), channel_id=1, source_target_pairs={{0,12},{1,13},{2,14},{3,15},{4,8},{5,9},{6,10},{7,11},{8,4},{9,5},... | collective-permute-start | bytes 1572872 | tf_op jit(solution)/shard_map/ppermute | solution.py:20
  24.8 14.6 %collective-permute-start.7 = (bf16[2,256,512]{2,1,0:T(8,128)(2,1)S(1)}, bf16[2,256,512]{2,1,0:T(8,128)(2,1)S(1)}, u32[]{:S(2)}, u32[]{:S(2)}) collective-permute-start(bf16[2,256,512]{2,1,0:T(8,128)(2,1)S(1)} %get-tuple-element.48.refs_0_), channel_id=1, source_target_pairs={{0,4},{1,5},{2,6},{3,7},{4,0},{5,1},{6,2},{7,3},{8,12},{9,13},{10,... | collective-permute-start | bytes 1572872 | tf_op jit(solution)/shard_map/ppermute | solution.py:20
  25.7 8.5 %collective-permute-start.6 = (f32[16,256]{1,0:T(8,128)S(1)}, f32[16,256]{1,0:T(8,128)S(1)}, u32[]{:S(2)}, u32[]{:S(2)}) collective-permute-start(f32[16,256]{1,0:T(8,128)S(1)} %get-tuple-element.47), channel_id=1, source_target_pairs={{0,192},{16,208},{32,224},{48,240},{64,128},{80,144},{96,160},{112... | collective-permute-start | bytes 49160 | tf_op jit(solution)/shard_map/ppermute | solution.py:20
  31.8 7.6 %collective-permute-start.4 = (f32[16,256]{1,0:T(8,128)S(1)}, f32[16,256]{1,0:T(8,128)S(1)}, u32[]{:S(2)}, u32[]{:S(2)}) collective-permute-start(f32[16,256]{1,0:T(8,128)S(1)} %get-tuple-element.47), channel_id=1, source_target_pairs={{0,64},{16,80},{32,96},{48,112},{64,0},{80,16},{96,32},{112,48},{1... | collective-permute-start | bytes 49160 | tf_op jit(solution)/shard_map/ppermute | solution.py:20
  39.5 6.5 %collective-permute-start.10 = (bf16[256,512]{1,0:T(8,128)(2,1)S(1)}, bf16[256,512]{1,0:T(8,128)(2,1)S(1)}, u32[]{:S(2)}, u32[]{:S(2)}) collective-permute-start(bf16[256,512]{1,0:T(8,128)(2,1)S(1)} %get-tuple-element.53), channel_id=1, source_target_pairs={{0,4},{1,5},{2,6},{3,7},{4,0},{5,1},{6,2},{7,3},{8,12},{9,13},{10,... | collective-permute-start | bytes 786440 | tf_op jit(solution)/shard_map/ppermute | solution.py:20
  40.7 7.7 %collective-permute-start.9 = (bf16[256,512]{1,0:T(8,128)(2,1)S(1)}, bf16[256,512]{1,0:T(8,128)(2,1)S(1)}, u32[]{:S(2)}, u32[]{:S(2)}) collective-permute-start(bf16[256,512]{1,0:T(8,128)(2,1)S(1)} %get-tuple-element.49.refs_0_), channel_id=1, source_target_pairs={{0,12},{1,13},{2,14},{3,15},{4,8},{5,9},{6,10},{7,11},{8,4},{9,5},... | collective-permute-start | bytes 786440 | tf_op jit(solution)/shard_map/ppermute | solution.py:20
  48.5 4.4 %collective-permute-start.11 = (bf16[8,256,512]{2,1,0:T(8,128)(2,1)S(1)}, bf16[8,256,512]{2,1,0:T(8,128)(2,1)S(1)}, u32[]{:S(2)}, u32[]{:S(2)}) collective-permute-start(bf16[8,256,512]{2,1,0:T(8,128)(2,1)S(1)} %stack_arrived.1.own_ref.refs_6_), channel_id=1, source_target_pairs={{0,1},{1,0},{2,3},{3,2},{4,5},{5,4},{6,7},{7,6},{8,9},{9,8},{10,11... | collective-permute-start | bytes 6291464 | tf_op jit(solution)/shard_map/ppermute | solution.py:20
  73.0 12.9 %collective-permute-start.19 = (bf16[256,512]{1,0:T(8,128)(2,1)S(1)}, bf16[256,512]{1,0:T(8,128)(2,1)S(1)}, u32[]{:S(2)}, u32[]{:S(2)}) collective-permute-start(bf16[256,512]{1,0:T(8,128)(2,1)S(1)} %get-tuple-element.65), channel_id=1, source_target_pairs={{0,4},{1,5},{2,6},{3,7},{4,0},{5,1},{6,2},{7,3},{8,12},{9,13},{10,... | collective-permute-start | bytes 786440 | tf_op jit(solution)/shard_map/ppermute | solution.py:20
  73.1 12.8 %collective-permute-start.20 = (bf16[256,512]{1,0:T(8,128)(2,1)S(1)}, bf16[256,512]{1,0:T(8,128)(2,1)S(1)}, u32[]{:S(2)}, u32[]{:S(2)}) collective-permute-start(bf16[256,512]{1,0:T(8,128)(2,1)S(1)} %get-tuple-element.66), channel_id=1, source_target_pairs={{0,12},{1,13},{2,14},{3,15},{4,8},{5,9},{6,10},{7,11},{8,4},{9,5},... | collective-permute-start | bytes 786440 | tf_op jit(solution)/shard_map/ppermute | solution.py:20
  76.0 7.2 %collective-permute-start.14 = (f32[40,256]{1,0:T(8,128)S(1)}, f32[40,256]{1,0:T(8,128)S(1)}, u32[]{:S(2)}, u32[]{:S(2)}) collective-permute-start(f32[40,256]{1,0:T(8,128)S(1)} %copy-done.12), channel_id=1, source_target_pairs={{0,48},{16,32},{32,16},{48,0},{64,112},{80,96},{96,80},{112,64},{1... | collective-permute-start | bytes 122888 | tf_op jit(solution)/shard_map/ppermute | solution.py:20
  77.9 7.4 %collective-permute-start.13 = (f32[40,256]{1,0:T(8,128)S(1)}, f32[40,256]{1,0:T(8,128)S(1)}, u32[]{:S(2)}, u32[]{:S(2)}) collective-permute-start(f32[40,256]{1,0:T(8,128)S(1)} %copy-done.12), channel_id=1, source_target_pairs={{0,32},{16,48},{32,0},{48,16},{64,96},{80,112},{96,64},{112,80},{1... | collective-permute-start | bytes 122888 | tf_op jit(solution)/shard_map/ppermute | solution.py:20
  78.9 6.4 %collective-permute-start.12 = (f32[40,256]{1,0:T(8,128)S(1)}, f32[40,256]{1,0:T(8,128)S(1)}, u32[]{:S(2)}, u32[]{:S(2)}) collective-permute-start(f32[40,256]{1,0:T(8,128)S(1)} %copy-done.12), channel_id=1, source_target_pairs={{0,16},{16,0},{32,48},{48,32},{64,80},{80,64},{96,112},{112,96},{1... | collective-permute-start | bytes 122888 | tf_op jit(solution)/shard_map/ppermute | solution.py:20
  86.1 14.6 %collective-permute-start.21 = (bf16[2,256,512]{2,1,0:T(8,128)(2,1)S(1)}, bf16[2,256,512]{2,1,0:T(8,128)(2,1)S(1)}, u32[]{:S(2)}, u32[]{:S(2)}) collective-permute-start(bf16[2,256,512]{2,1,0:T(8,128)(2,1)S(1)} %get-tuple-element.67), channel_id=1, source_target_pairs={{0,4},{1,5},{2,6},{3,7},{4,0},{5,1},{6,2},{7,3},{8,12},{9,13},{10,... | collective-permute-start | bytes 1572872 | tf_op jit(solution)/shard_map/ppermute | solution.py:20
  87.4 13.7 %collective-permute-start.22 = (bf16[2,256,512]{2,1,0:T(8,128)(2,1)S(1)}, bf16[2,256,512]{2,1,0:T(8,128)(2,1)S(1)}, u32[]{:S(2)}, u32[]{:S(2)}) collective-permute-start(bf16[2,256,512]{2,1,0:T(8,128)(2,1)S(1)} %get-tuple-element.68), channel_id=1, source_target_pairs={{0,12},{1,13},{2,14},{3,15},{4,8},{5,9},{6,10},{7,11},{8,4},{9,5},... | collective-permute-start | bytes 1572872 | tf_op jit(solution)/shard_map/ppermute | solution.py:20
  88.1 10.6 %collective-permute-start.17 = (f32[40,256]{1,0:T(8,128)S(1)}, f32[40,256]{1,0:T(8,128)S(1)}, u32[]{:S(2)}, u32[]{:S(2)}) collective-permute-start(f32[40,256]{1,0:T(8,128)S(1)} %get-tuple-element.61.refs_0_.whole_ref), channel_id=1, source_target_pairs={{0,192},{16,208},{32,224},{48,240},{64,128},{80,144},{96,160},{112... | collective-permute-start | bytes 122888 | tf_op jit(solution)/shard_map/ppermute | solution.py:20
  90.7 8.0 %collective-permute-start.16 = (f32[40,256]{1,0:T(8,128)S(1)}, f32[40,256]{1,0:T(8,128)S(1)}, u32[]{:S(2)}, u32[]{:S(2)}) collective-permute-start(f32[40,256]{1,0:T(8,128)S(1)} %get-tuple-element.61.refs_0_.whole_ref), channel_id=1, source_target_pairs={{0,128},{16,144},{32,160},{48,176},{64,192},{80,208},{96,224},{112... | collective-permute-start | bytes 122888 | tf_op jit(solution)/shard_map/ppermute | solution.py:20
  91.4 9.3 %collective-permute-start.15 = (f32[40,256]{1,0:T(8,128)S(1)}, f32[40,256]{1,0:T(8,128)S(1)}, u32[]{:S(2)}, u32[]{:S(2)}) collective-permute-start(f32[40,256]{1,0:T(8,128)S(1)} %get-tuple-element.61.refs_0_.whole_ref), channel_id=1, source_target_pairs={{0,64},{16,80},{32,96},{48,112},{64,0},{80,16},{96,32},{112,48},{1... | collective-permute-start | bytes 122888 | tf_op jit(solution)/shard_map/ppermute | solution.py:20
  101.2 15.0 %collective-permute-start.23 = (bf16[256,512]{1,0:T(8,128)(2,1)S(1)}, bf16[256,512]{1,0:T(8,128)(2,1)S(1)}, u32[]{:S(2)}, u32[]{:S(2)}) collective-permute-start(bf16[256,512]{1,0:T(8,128)(2,1)S(1)} %get-tuple-element.70), channel_id=1, source_target_pairs={{0,2},{1,3},{2,0},{3,1},{4,6},{5,7},{6,4},{7,5},{8,10},{9,11},{10,... | collective-permute-start | bytes 786440 | tf_op jit(solution)/shard_map/ppermute | solution.py:20
  113.4 7.9 %collective-permute-start.24 = (bf16[256,512]{1,0:T(8,128)(2,1)S(1)}, bf16[256,512]{1,0:T(8,128)(2,1)S(1)}, u32[]{:S(2)}, u32[]{:S(2)}) collective-permute-start(bf16[256,512]{1,0:T(8,128)(2,1)S(1)} %slice_bitcast_fusion), channel_id=1, source_target_pairs={{0,128},{16,144},{32,160},{48,176},{64,192},{80,208},{96,224},{112... | collective-permute-start | bytes 786440 | tf_op jit(solution)/shard_map/ppermute | solution.py:20
  (25 other events, 224.6 us)
Sparse Core Ops, SparseCore 0:
  56.0 56.3 reduce-scatter.1
